TPU v7x, 256 devices: a whole 4x4x8 slice. The times are simulated.
256 devices in a mesh: ex: 64 (over z, y, x_hi), feat: 4 (over x_lo, core).
Axes of the slice: x: 4 (x_hi: 2, x_lo: 2; x = x_hi * 2 + x_lo), y: 4, z: 8, core: 2. Of those that a mesh axis runs over, the one named last changes fastest.
Arguments:
- left_factors: bfloat16 [4, 1664, 4, 5120], P('feat', 'ex'), may hold values from -6 to 6
- right_factors: bfloat16 [4, 1664, 4, 5120], P('feat', 'ex'), may hold values from -6 to 6
- left_proj: bfloat16 [4, 5120, 32], P('feat'), may hold values from -0.078125 to 0.078125
- right_proj: bfloat16 [4, 5120, 64], P('feat'), may hold values from -0.078125 to 0.078125
- val_ids: int32 [256], replicated, may hold values from 0 to 1663
Outputs:
- weights: float32 [1664], P('ex')
- residual: float32 [1664], P('ex')
Inputs may be any that keep to these rules, and one draw needn't show every extreme that they name: `val_ids`: ids of training examples; an id may repeat.
All inputs are finite; a program needn't handle non-finite values.
Results may differ from a plain program's by a relative error of at most 0.03.
Values may be sent and summed in bfloat16 or wider, within the bound.
A program may use at most 64 MiB of HBM per device.

v0:
```python
import math

import jax
import jax.numpy as jnp
from jax import lax
from jax.sharding import PartitionSpec as P

ITERS = 2


RIDGE = 0.5


def inner_sum(value):
    return lax.psum(value, "ex")


def per_device(left_factors, right_factors, left_proj, right_proj, val_ids):
    local_layers, rows, rank, width = left_factors.shape
    left_part = jnp.einsum(
        "erd,dk->erk", left_factors[0], left_proj[0], preferred_element_type=jnp.float32
    )
    right_part = jnp.einsum(
        "erd,dk->erk", right_factors[0], right_proj[0], preferred_element_type=jnp.float32
    )
    outer = jnp.einsum(
        "erk,erm->ekm", left_part, right_part, preferred_element_type=jnp.float32
    ) / math.sqrt(rank)
    blocks = outer.reshape(rows, -1)
    features = blocks.astype(jnp.bfloat16)
    total_features = features.shape[1] * lax.axis_size("feat")
    wide = features.astype(jnp.float32)
    row_ids = lax.axis_index("ex") * rows + jnp.arange(rows, dtype=jnp.int32)
    counts = jnp.sum((val_ids[:, None] == row_ids[None, :]).astype(jnp.float32), axis=0)
    val_count = val_ids.shape[0]
    target = lax.psum(jnp.dot(counts, wide, precision=lax.Precision.HIGHEST), "ex") / val_count
    align_part = jnp.dot(wide, target, precision=lax.Precision.HIGHEST) * math.sqrt(
        val_count / total_features
    )
    partial_gram = lax.dot_general(
        features,
        lax.all_gather(features, "ex", axis=0, tiled=True),
        (((1,), (1,)), ((), ())),
        preferred_element_type=jnp.float32,
    )
    gram, align = lax.psum((partial_gram, align_part), "feat")
    weights = jnp.zeros_like(align)
    residual = align
    direction = align
    norm_now = inner_sum(jnp.sum(residual * residual))
    for step in range(ITERS):
        whole = lax.all_gather(direction, "ex", axis=0, tiled=True)
        image = (
            jnp.dot(gram, whole, precision=lax.Precision.HIGHEST) / total_features
            + RIDGE * direction
        )
        alpha = norm_now / inner_sum(jnp.sum(direction * image))
        weights = weights + alpha * direction
        residual = residual - alpha * image
        norm_next = inner_sum(jnp.sum(residual * residual))
        direction = residual + norm_next / norm_now * direction
        norm_now = norm_next
    return (weights, residual)


def solution(mesh):
    return jax.shard_map(
        per_device,
        mesh=mesh,
        in_specs=(
            P("feat", "ex", None, None),
            P("feat", "ex", None, None),
            P("feat", None, None),
            P("feat", None, None),
            P(),
        ),
        out_specs=(P("ex"), P("ex")),
        check_vma=False,
    )
```

profile of v0, /device:TPU:4, one launch (start us, length us, event | category | flops | bytes accessed | tf_op | source)
XLA Modules:
  0.0 1136.7 jit_solution(14582565477035458492)
XLA Ops:
  7.2 0.0 copy-start
  7.2 0.0 copy-start.2
  7.2 0.0 copy-start.3
  7.2 0.0 all-gather.3.cloned.1.call-start
  7.2 1.0 copy-done
  8.3 1.7 fusion
  10.0 0.0 copy-done.2
  10.0 0.0 copy-done.3
  10.0 0.0 copy-start.4
  10.0 0.0 copy-start.1
  10.0 0.5 fusion.2
  10.6 0.3 fusion.4
  10.8 0.9 reshape.17
  11.7 0.0 all-gather.3.cloned.1.call-update
  11.7 0.0 all-reduce.5.cloned.1.call-start
  11.7 0.2 convert_element_type.11
  12.0 0.0 copy-done.4
  12.0 0.6 dynamic-slice
  13.2 0.0 copy-done.1
  13.2 0.2 convert_reduce_fusion
  13.4 0.2 fusion.14
  13.6 183.8 %psum.49 = f32[2048]{0:T(1024)S(1)} all-reduce(f32[2048]{0:T(1024)S(1)} %bitcast.41), channel_id=1, replica_groups=mesh['ex'=64,'feat'=4] {'ex'}, use_global_device_ids=true, to_apply=%region_1.0 | all-reduce | flops 2048 | bytes 16384 | tf_op jit(solution)/shard_map/psum | solution.py:36
  197.4 0.0 all-gather.3.cloned.1.call-done
  197.4 9.1 reshape.18
  206.5 5.8 fusion.17
  212.2 0.0 all-reduce.5.cloned.1.call-update
  212.3 0.2 fusion.9
  212.4 5.7 psum.50
  218.1 0.3 dynamic-update-slice
  218.4 185.9 %all-reduce = f32[1664]{0:T(1024)S(1)} all-reduce(f32[1664]{0:T(1024)S(1)} %dynamic-update-slice), channel_id=1, replica_groups=mesh['ex'=64,'feat'=4] {'ex'}, use_global_device_ids=true, to_apply=%add | all-reduce | flops 1664 | bytes 13312
  404.3 0.0 all-reduce.5.cloned.1.call-done
  404.4 1.9 multiply_reduce_fusion.2
  406.2 177.0 %all-reduce.2 = (f32[]{:T(128)}, f32[]{:T(128)}) all-reduce(f32[]{:T(128)} %get-tuple-element.3, f32[]{:T(128)} %get-tuple-element.2), channel_id=1, replica_groups=mesh['ex'=64,'feat'=4] {'ex'}, use_global_device_ids=true, to_apply=%region_4.0 | all-reduce | flops 2 | bytes 16 | tf_op jit(solution)/shard_map/psum | solution.py:15
  584.5 0.6 multiply_reduce_fusion.1
  585.1 180.6 %psum.54 = f32[]{:T(128)} all-reduce(f32[]{:T(128)} %get-tuple-element.8), channel_id=1, replica_groups=mesh['ex'=64,'feat'=4] {'ex'}, use_global_device_ids=true, to_apply=%region_9.0 | all-reduce | flops 1 | bytes 8 | tf_op jit(solution)/shard_map/psum | solution.py:15
  767.0 0.1 fusion.16
  767.1 178.5 %all-reduce.1 = f32[1664]{0:T(1024)S(1)} all-reduce(f32[1664]{0:T(1024)S(1)} %get-tuple-element.6), channel_id=1, replica_groups=mesh['ex'=64,'feat'=4] {'ex'}, use_global_device_ids=true, to_apply=%add.1 | all-reduce | flops 1664 | bytes 13312
  945.7 1.8 multiply_reduce_fusion
  947.5 180.5 %psum.55 = f32[]{:T(128)} all-reduce(f32[]{:T(128)} %get-tuple-element.11), channel_id=1, replica_groups=mesh['ex'=64,'feat'=4] {'ex'}, use_global_device_ids=true, to_apply=%region_11.0 | all-reduce | flops 1 | bytes 8 | tf_op jit(solution)/shard_map/psum | solution.py:15
  1129.4 0.5 multiply_subtract_fusion
  (6 shorter events, 0.0 us)
Async XLA Ops:
  7.2 1.1 copy-start
  7.2 2.8 copy-start.2
  7.2 2.8 copy-start.3
  7.2 190.2 %all-gather.3.cloned.1.call-start = ((), (), s32[]{:S(2)}) async-start(), calls=%async_computation.1 | async-start | bytes 8519680 | tf_op jit(solution)/shard_map/all_gather | solution.py:42
  10.0 1.9 copy-start.4
  10.0 3.2 copy-start.1
  11.7 392.6 %all-reduce.5.cloned.1.call-start = ((), (), s32[]{:S(2)}) async-start(), calls=%async_computation | async-start | bytes 425984 | tf_op jit(solution)/shard_map/psum | solution.py:46
Sparse Core Ops, SparseCore 0:
  11.8 154.2 all-gather.2
  212.4 39.9 all-reduce.4
where the time goes:
time: 1140 us
  blocking collectives  1090 us (96%)
  between operations  18.7 us (2%)
  matrix products  12.3 us (1%)
  local copies, waits for them, and re-layouts  12.1 us (1%)
    psum x3, blocking collectives, inner_sum(): return lax.psum(value, 'ex')  538 us
    unnamed x2, blocking collectives  364 us
    psum x1, blocking collectives, per_device(): lax.psum(jnp.dot(counts, wide, precision=lax.Precision.HIGHEST), 'ex')  184 us
  transfers between devices with their start and end apart: 2, of which 0 were waited for; matrix products, arithmetic and copies ran while one was open for 0% of the time, Pallas kernels for 0%

commit v1 on v0

v1 whole, which is shorter than its diff:
```python
import functools
import math

import jax
import jax.numpy as jnp
from jax import lax
from jax.experimental import pallas as pl
from jax.experimental.pallas import tpu as pltpu
from jax.sharding import PartitionSpec as P

MESH = pl.DeviceIdType.MESH
NT = (((1,), (1,)), ((), ()))
NN = (((1,), (0,)), ((), ()))
SIZE = dict(z=8, y=4, xh=2, xl=2, c=2)
RIDGE = 0.5
CHUNKS = 4
LANES = 128


def coordinates():
    ex = lax.axis_index("ex")
    feat = lax.axis_index("feat")
    return dict(z=ex // 8, y=(ex // 2) % 4, xh=ex % 2, xl=feat // 2, c=feat % 2)


def device(at):
    return (at["z"] * 8 + at["y"] * 2 + at["xh"], at["xl"] * 2 + at["c"])


def moved(at, **steps):
    new = dict(at)
    for axis, step in steps.items():
        if step:
            new[axis] = (at[axis] + step) % SIZE[axis]
    return new


def hops(y, xh, xl):
    x = 2 * xh + xl
    return min(y, 4 - y) + min(x, 4 - x)


def split(value):
    high = value.astype(jnp.bfloat16)
    low = (value - high.astype(jnp.float32)).astype(jnp.bfloat16)
    return high, low


def pack(value):
    return jnp.concatenate([value[:16], value[16:]], axis=1)


def unpack(value):
    return jnp.concatenate([value[:, :64], value[:, 64:]], axis=0)


def dot(a, b, dims):
    return lax.dot_general(a, b, dims, preferred_element_type=jnp.float32)


def to_features(left, right, vector):
    both = jnp.concatenate(split(left.astype(jnp.float32) * vector), axis=0)
    sums = dot(both, right, NT)
    return pack(sums[:32] + sums[32:])


def kernel(
    rows, rank, total_features, val_count,
    lf_hbm, rf_hbm, lp_hbm, rp_hbm, ids_hbm, out_ref,
    lf, rf, lp, rp, ids, blocks, first, second, sums, pair,
    load_sem, ids_sem, send_sem, recv_sem,
):
    at = coordinates()
    width = lf_hbm.shape[3]
    step = width // CHUNKS
    used = rows * rank
    plane_slot = at["y"] * 2 + at["xh"]
    slot = at["xl"] * 8 + plane_slot

    loads = []
    for i in range(CHUNKS):
        part = pl.ds(i * step, step)
        group = [
            pltpu.make_async_copy(lp_hbm.at[0, :, part], lp.at[:, part], load_sem.at[i, 0]),
            pltpu.make_async_copy(lf_hbm.at[0, :, :, part], lf.at[i], load_sem.at[i, 1]),
            pltpu.make_async_copy(rp_hbm.at[0, :, part], rp.at[:, part], load_sem.at[i, 2]),
            pltpu.make_async_copy(rf_hbm.at[0, :, :, part], rf.at[i], load_sem.at[i, 3]),
        ]
        for copy in group:
            copy.start()
        loads.append(group)
    load_ids = pltpu.make_async_copy(ids_hbm, ids, ids_sem)
    load_ids.start()

    along_z = [moved(at, z=d) for d in (4, 3, 5, 2, 6, 1, 7)]
    plane = [(y, xh, xl) for y in range(4) for xh in range(2) for xl in range(2) if y or xh or xl]
    plane = [moved(at, y=y, xh=xh, xl=xl) for y, xh, xl in sorted(plane, key=lambda o: -hops(*o))]
    other = moved(at, c=1)
    barrier = pltpu.get_barrier_semaphore()
    for peer in along_z + plane + [other]:
        pl.semaphore_signal(barrier, inc=1, device_id=device(peer), device_id_type=MESH)

    lane = lax.broadcasted_iota(jnp.int32, (8, LANES), 1)
    own_id = jnp.where(lane < used, (at["z"] * 8 + plane_slot) * rows + lane // rank, -1)
    load_ids.wait()

    def count(i, total):
        for j in range(8):
            total = total + jnp.where(own_id == ids[i * 8 + j], 1.0, 0.0)
        return total

    counts = lax.fori_loop(0, val_count // 8, count, jnp.zeros((8, LANES), jnp.float32))[:1]

    left_part = jnp.zeros((32, used), jnp.float32)
    right_part = jnp.zeros((64, used), jnp.float32)
    for i in range(CHUNKS):
        for copy in loads[i]:
            copy.wait()
        part = slice(i * step, (i + 1) * step)
        left_part += dot(lp[:, part], lf[i].reshape(used, step), NT)
        right_part += dot(rp[:, part], rf[i].reshape(used, step), NT)
    own = jnp.concatenate([left_part, right_part], axis=0).astype(jnp.bfloat16)
    own = jnp.concatenate([own, jnp.zeros((96, LANES - used), jnp.bfloat16)], axis=1)
    blocks[slot] = own

    def sends(stage, buffer, index, peers):
        for peer in peers:
            pltpu.make_async_remote_copy(
                src_ref=buffer.at[index], dst_ref=buffer.at[index],
                send_sem=send_sem.at[stage], recv_sem=recv_sem.at[stage],
                device_id=device(peer), device_id_type=MESH,
            ).start()

    def all_of(stage, buffer, number):
        view = buffer.at[pl.ds(0, number)]
        return pltpu.make_async_remote_copy(
            src_ref=view, dst_ref=view, send_sem=send_sem.at[stage], recv_sem=recv_sem.at[stage],
            device_id=device(other), device_id_type=MESH,
        )

    first[at["z"]] = to_features(own[:32], own[32:], counts)
    pl.semaphore_wait(barrier, len(along_z) + len(plane) + 1)
    sends(0, first, at["z"], along_z)
    sends(1, blocks, slot, plane)
    all_of(0, first, 7).wait_recv()
    second[slot] = jnp.sum(first[...], axis=0)
    sends(2, second, slot, plane)
    all_of(1, blocks, 15).wait_recv()
    left = [jnp.concatenate([blocks[8 * l + b, :32] for b in range(8)], axis=1) for l in range(2)]
    right = [jnp.concatenate([blocks[8 * l + b, 32:] for b in range(8)], axis=1) for l in range(2)]
    all_of(2, second, 15).wait_recv()
    target = [jnp.sum(second[pl.ds(8 * l, 8)], axis=0) for l in range(2)]

    def to_examples(values, index):
        total = jnp.zeros((32, 8 * LANES), jnp.float32)
        squares = jnp.zeros((16, LANES), jnp.float32)
        for l in range(2):
            both = jnp.concatenate(split(unpack(values[l])), axis=0)
            mixed = dot(both, right[l], NN)
            total += (mixed[:32] + mixed[32:]) * left[l].astype(jnp.float32)
            squares += values[l] * values[l]
        parts = [jnp.sum(total[:, b * LANES:(b + 1) * LANES], axis=0, keepdims=True) for b in range(8)]
        mine = pair.at[index, at["c"]]
        mine[...] = jnp.concatenate(parts + [jnp.sum(squares, axis=0, keepdims=True)], axis=0)
        sends(3 + index, pair.at[index], at["c"], [other])
        all_of(3 + index, pair.at[index], 1).wait_recv()
        both = pair[index, 0] + pair[index, 1]
        each = both[:8]
        each = each + jnp.where(lane % 2 == 0, pltpu.roll(each, LANES - 1, 1), pltpu.roll(each, 1, 1))
        each = each + jnp.where(lane % 4 < 2, pltpu.roll(each, LANES - 2, 1), pltpu.roll(each, 2, 1))
        return each, jnp.sum(both[8:9], axis=1, keepdims=True)

    def to_all_features(vector, index, extra):
        row = jnp.concatenate([vector[b:b + 1] for b in range(8)], axis=1)
        parts = [to_features(left[l], right[l], row) for l in range(2)]
        parts += [jnp.sum(e, axis=0, keepdims=True) for e in extra]
        sums[index, at["z"]] = jnp.concatenate(parts, axis=0)
        sends(6 + index, sums.at[index], at["z"], along_z)
        all_of(6 + index, sums.at[index], 7).wait_recv()
        whole = jnp.sum(sums[index], axis=0)
        scalars = [jnp.sum(whole[32 + i:33 + i], axis=1, keepdims=True) * (1.0 / rank) for i in range(2)]
        return [whole[:16], whole[16:32]], scalars

    scale = 1.0 / (rank * total_features)
    align, _ = to_examples(target, 0)
    residual = align * (math.sqrt(val_count / total_features) / (val_count * rank))
    start = residual
    mixed, (norm, _) = to_all_features(residual, 0, [residual * residual, jnp.zeros_like(residual)])
    image, square = to_examples(mixed, 1)
    image = image * scale + RIDGE * start
    alpha = norm / (square * scale + RIDGE * norm)
    weights = alpha * start
    residual = start - alpha * image
    again, (norm_next, cross) = to_all_features(residual, 1, [residual * residual, residual * start])
    beta = norm_next / norm
    direction = residual + beta * start
    mixed = [again[l] + beta * mixed[l] for l in range(2)]
    image, square = to_examples(mixed, 2)
    image = image * scale + RIDGE * direction
    length = norm_next + 2.0 * beta * cross + beta * beta * norm
    alpha = norm_next / (square * scale + RIDGE * length)
    weights = weights + alpha * direction
    residual = residual - alpha * image

    mine = lax.broadcasted_iota(jnp.int32, (8, LANES), 0) == plane_slot
    pieces = []
    for value in (weights, residual):
        value = jnp.sum(jnp.where(mine, value, 0.0), axis=0, keepdims=True)
        for _ in range(3):
            high = value.astype(jnp.bfloat16)
            pieces.append(high.astype(jnp.float32))
            value = value - high.astype(jnp.float32)
    pieces.append(jnp.zeros((2, LANES), jnp.float32))
    take = (
        lax.broadcasted_iota(jnp.int32, (LANES, LANES), 0)
        == rank * lax.broadcasted_iota(jnp.int32, (LANES, LANES), 1)
    )
    taken = dot(
        jnp.concatenate(pieces, axis=0).astype(jnp.bfloat16),
        jnp.where(take, 1.0, 0.0).astype(jnp.bfloat16), NN,
    )
    out_ref[0:1] = taken[0:1] + taken[1:2] + taken[2:3]
    out_ref[1:2] = taken[3:4] + taken[4:5] + taken[5:6]

    all_of(0, first, 7).wait_send()
    all_of(1, blocks, 15).wait_send()
    all_of(2, second, 15).wait_send()
    for i in range(3):
        all_of(3 + i, pair.at[i], 1).wait_send()
    for i in range(2):
        all_of(6 + i, sums.at[i], 7).wait_send()


def per_device(left_factors, right_factors, left_proj, right_proj, val_ids):
    _, rows, rank, width = left_factors.shape
    left_proj = jnp.swapaxes(left_proj, 1, 2)
    right_proj = jnp.swapaxes(right_proj, 1, 2)
    ka, kb = left_proj.shape[1], right_proj.shape[1]
    val_count = val_ids.shape[0]
    total_features = ka * kb * lax.axis_size("feat")
    step = width // CHUNKS
    out = pl.pallas_call(
        functools.partial(kernel, rows, rank, total_features, val_count),
        out_shape=jax.ShapeDtypeStruct((2, LANES), jnp.float32),
        in_specs=[pl.BlockSpec(memory_space=pltpu.HBM)] * 5,
        out_specs=pl.BlockSpec(memory_space=pltpu.VMEM),
        scratch_shapes=[
            pltpu.VMEM((CHUNKS, rows, rank, step), jnp.bfloat16),
            pltpu.VMEM((CHUNKS, rows, rank, step), jnp.bfloat16),
            pltpu.VMEM((ka, width), jnp.bfloat16),
            pltpu.VMEM((kb, width), jnp.bfloat16),
            pltpu.SMEM((val_count,), jnp.int32),
            pltpu.VMEM((16, ka + kb, LANES), jnp.bfloat16),
            pltpu.VMEM((8, 16, LANES), jnp.float32),
            pltpu.VMEM((16, 16, LANES), jnp.float32),
            pltpu.VMEM((2, 8, 34, LANES), jnp.float32),
            pltpu.VMEM((3, 2, 9, LANES), jnp.float32),
            pltpu.SemaphoreType.DMA((CHUNKS, 4)),
            pltpu.SemaphoreType.DMA,
            pltpu.SemaphoreType.DMA((8,)),
            pltpu.SemaphoreType.DMA((8,)),
        ],
        compiler_params=pltpu.CompilerParams(
            collective_id=0, has_side_effects=True, vmem_limit_bytes=56 * 2**20
        ),
        name="reweight",
    )(left_factors, right_factors, left_proj, right_proj, val_ids)
    return out[0, :rows], out[1, :rows]


def solution(mesh):
    return jax.shard_map(
        per_device,
        mesh=mesh,
        in_specs=(
            P("feat", "ex", None, None),
            P("feat", "ex", None, None),
            P("feat", None, None),
            P("feat", None, None),
            P(),
        ),
        out_specs=(P("ex"), P("ex")),
        check_vma=False,
    )
```

time: 1140 us -> 37.9 us (0.03)
  the two profiles are of different devices: /device:TPU:4 before, /device:TPU:1 now
where the time goes in v1:
time: 37.9 us; the launch traced here: 37.8 us
  Pallas kernels  35.9 us (95%)
  local copies, waits for them, and re-layouts  1.25 us (3%)
  between operations  0.64 us (2%)
    pallas_call x1, Pallas kernels, per_device(): pl.pallas_call(functools.partial(kernel, rows, rank, total_features, val_...  35.9 us
    squeeze x1, local copies, waits for them, and re-layouts, per_device(): return (out[0, :rows], out[1, :rows])  1.25 us

profile of v1, /device:TPU:1, one launch (start us, length us, event | category | flops | bytes accessed | tf_op | source)
XLA Modules:
  0.0 37.8 jit_solution(14475201851395174534)
XLA Ops:
  0.6 35.9 %reweight.1 = f32[2,128]{1,0:T(2,128)} custom-call(bf16[1,26,4,5120]{3,2,1,0:T(4,128)(2,1)} %lf_hbm.1, bf16[1,26,4,5120]{3,2,1,0:T(4,128)(2,1)} %rf_hbm.1, bf16[1,32,5120]{2,1,0:T(8,128)(2,1)} %bitcast.7, bf16[1,64,5120]{2,1,0:T(8,128)(2,1)} %bitcast.6, s32[256]{0:T(256)} %ids_hbm.1), custom_call_target="tpu_custom_call" | custom-call | tf_op jit(solution)/shard_map/reweight/pallas_call | solution.py:242
  36.5 1.3 %slice_bitcast_fusion = (f32[26]{0:T(128)}, f32[26]{0:T(128)}) fusion(f32[2,128]{1,0:T(2,128)} %reweight.1), kind=kLoop, calls=%fused_computation | loop fusion | bytes 416 | tf_op jit(solution)/shard_map/squeeze | solution.py:268

commit v2 on v1

v2 whole, which is shorter than its diff:
```python
import functools
import math

import jax
import jax.numpy as jnp
from jax import lax
from jax.experimental import pallas as pl
from jax.experimental.pallas import tpu as pltpu
from jax.sharding import PartitionSpec as P

MESH = pl.DeviceIdType.MESH
NT = (((1,), (1,)), ((), ()))
NN = (((1,), (0,)), ((), ()))
SIZE = dict(z=8, y=4, xh=2, xl=2, c=2)
RIDGE = 0.5
CHUNKS = 4
LANES = 128
GROUP = 32


def coordinates():
    ex = lax.axis_index("ex")
    feat = lax.axis_index("feat")
    return dict(z=ex // 8, y=(ex // 2) % 4, xh=ex % 2, xl=feat // 2, c=feat % 2)


def device(at):
    return (at["z"] * 8 + at["y"] * 2 + at["xh"], at["xl"] * 2 + at["c"])


def moved(at, **steps):
    new = dict(at)
    for axis, step in steps.items():
        if not (isinstance(step, int) and step == 0):
            new[axis] = (at[axis] + step) % SIZE[axis]
    return new


def hops(y, xh, xl):
    x = 2 * xh + xl
    return min(y, 4 - y) + min(x, 4 - x)


def split(value):
    high = value.astype(jnp.bfloat16)
    low = (value - high.astype(jnp.float32)).astype(jnp.bfloat16)
    return jnp.concatenate([high, low], axis=0)


def pack(value):
    return jnp.concatenate([value[:16], value[16:]], axis=1)


def unpack(value):
    return jnp.concatenate([value[:, :64], value[:, 64:]], axis=0)


def dot(a, b, dims):
    return lax.dot_general(a, b, dims, preferred_element_type=jnp.float32)


def to_features(left, right, row):
    sums = dot(split(left.astype(jnp.float32) * row), right, NT)
    return pack(sums[:32] + sums[32:])


def to_lanes(left, right, values):
    total = None
    for l in range(2):
        mixed = dot(split(unpack(values[l])), right[l], NN)
        term = (mixed[:32] + mixed[32:]) * left[l].astype(jnp.float32)
        total = term if total is None else total + term
    return jnp.sum(total, axis=0, keepdims=True)


def rows_of(line):
    return jnp.concatenate([line[:, i:i + LANES] for i in range(0, line.shape[1], LANES)], axis=0)


def line_of(rows):
    return jnp.concatenate([rows[i:i + 1] for i in range(rows.shape[0])], axis=1)


def over_rank(rows):
    rows = rows + pltpu.roll(rows, 2 * GROUP, 1)
    return rows + pltpu.roll(rows, GROUP, 1)


def total(row):
    return jnp.sum(row, axis=1, keepdims=True)


def squares(values):
    return jnp.sum(values[0] * values[0] + values[1] * values[1], axis=0, keepdims=True)


def kernel(
    rows, rank, total_features, val_count,
    lf_hbm, rf_hbm, lp_hbm, rp_hbm, ids_hbm, out_ref,
    lf, rf, lp, rp, ids, blocks, first, second, sums, last, pair_0, pair_1, pair_2, pair_3,
    load_sem, ids_sem, send_sem, recv_sem,
):
    at = coordinates()
    width = lf_hbm.shape[3]
    step = width // CHUNKS
    used = rows * rank
    plane_slot = at["y"] * 2 + at["xh"]
    slot = at["xl"] * 8 + plane_slot
    two = at["z"] // 2
    sign = 2 * (at["z"] % 2) - 1

    along_z = [moved(at, z=d) for d in (4, 3, 5, 2, 6, 1, 7)]
    next_twos = [moved(at, z=sign * d + 8) for d in (3, 2, 1)]
    twin = moved(at, z=8 - sign)
    plane = [(y, xh, xl) for y in range(4) for xh in range(2) for xl in range(2) if y or xh or xl]
    plane = [moved(at, y=y, xh=xh, xl=xl) for y, xh, xl in sorted(plane, key=lambda o: -hops(*o))]
    other = moved(at, c=1)
    barrier = pltpu.get_barrier_semaphore()
    for peer in along_z + plane + [other]:
        pl.semaphore_signal(barrier, inc=1, device_id=device(peer), device_id_type=MESH)

    loads = []
    for i in range(CHUNKS):
        part = pl.ds(i * step, step)
        group = [
            pltpu.make_async_copy(lp_hbm.at[0, :, part], lp.at[:, part], load_sem.at[i, 0]),
            pltpu.make_async_copy(lf_hbm.at[0, :, :, part], lf.at[i], load_sem.at[i, 1]),
            pltpu.make_async_copy(rp_hbm.at[0, :, part], rp.at[:, part], load_sem.at[i, 2]),
            pltpu.make_async_copy(rf_hbm.at[0, :, :, part], rf.at[i], load_sem.at[i, 3]),
        ]
        for copy in group:
            copy.start()
        loads.append(group)
    load_ids = pltpu.make_async_copy(ids_hbm, ids, ids_sem)
    load_ids.start()

    lane = lax.broadcasted_iota(jnp.int32, (8, LANES), 1) % GROUP
    own_id = jnp.where(lane < rows, (at["z"] * 8 + plane_slot) * rows + lane, -1)
    load_ids.wait()

    def count(i, counts):
        for j in range(8):
            counts = counts + jnp.where(own_id == ids[i * 8 + j], 1.0, 0.0)
        return counts

    counts = lax.fori_loop(0, val_count // 8, count, jnp.zeros((8, LANES), jnp.float32))[:1]

    left_part = jnp.zeros((32, used), jnp.float32)
    right_part = jnp.zeros((64, used), jnp.float32)
    for i in range(CHUNKS):
        for copy in loads[i]:
            copy.wait()
        part = slice(i * step, (i + 1) * step)
        left_part += dot(lp[:, part], lf[i].reshape(used, step), NT)
        right_part += dot(rp[:, part], rf[i].reshape(used, step), NT)
    own = jnp.concatenate([left_part, right_part], axis=0).astype(jnp.bfloat16)
    source = lax.broadcasted_iota(jnp.int32, (used, LANES), 0)
    goal = lax.broadcasted_iota(jnp.int32, (used, LANES), 1)
    order = jnp.where((source // rank == goal % GROUP) & (source % rank == goal // GROUP), 1.0, 0.0)
    own = dot(own, order.astype(jnp.bfloat16), NN).astype(jnp.bfloat16)
    blocks[slot] = own

    def send(stage, source, goal, peers):
        for peer in peers:
            pltpu.make_async_remote_copy(
                src_ref=source, dst_ref=goal, send_sem=send_sem.at[stage], recv_sem=recv_sem.at[stage],
                device_id=device(peer), device_id_type=MESH,
            ).start()

    def all_of(stage, view):
        return pltpu.make_async_remote_copy(
            src_ref=view, dst_ref=view, send_sem=send_sem.at[stage], recv_sem=recv_sem.at[stage],
            device_id=device(other), device_id_type=MESH,
        )

    def share(stage, buffer, index, value, peers):
        buffer[index] = value
        send(stage, buffer.at[index], buffer.at[index], peers)

    def factors(base):
        left = [jnp.concatenate([blocks[base + 8 * l + b, :32] for b in range(8)], axis=1) for l in range(2)]
        right = [jnp.concatenate([blocks[base + 8 * l + b, 32:] for b in range(8)], axis=1) for l in range(2)]
        return left, right

    target = to_features(own[:32], own[32:], counts)
    pl.semaphore_wait(barrier, len(along_z) + len(plane) + 1)
    share(0, first, at["z"], target, along_z)
    send(1, blocks.at[slot], blocks.at[slot], plane)
    send(3, blocks.at[slot], blocks.at[16 + slot], [twin])
    all_of(0, first.at[pl.ds(0, 7)]).wait_recv()
    share(2, second, slot, jnp.sum(first[...], axis=0), plane)
    all_of(3, blocks.at[16 + slot]).wait_recv()
    send(4, blocks.at[16 + slot], blocks.at[16 + slot], plane)
    all_of(1, blocks.at[pl.ds(0, 15)]).wait_recv()
    all_of(2, second.at[pl.ds(0, 15)]).wait_recv()
    target = [jnp.sum(second[pl.ds(8 * l, 8)], axis=0) for l in range(2)]

    scale = 1.0 / (rank * total_features)
    align_scale = math.sqrt(val_count / total_features) / (val_count * rank)

    share(5, pair_0, at["c"], rows_of(to_lanes(*factors(0), target)), [other])
    all_of(5, pair_0.at[0]).wait_recv()
    start = over_rank(pair_0[0] + pair_0[1]) * align_scale

    left, right = factors(0)
    line = line_of(start)
    norm_row = jnp.sum(start * start, axis=0, keepdims=True)
    value = jnp.concatenate([to_features(left[l], right[l], line) for l in range(2)] + [norm_row], axis=0)
    share(9, sums, at["z"], value, along_z)

    all_of(4, blocks.at[pl.ds(16, 15)]).wait_recv()
    share(6, pair_1, at["c"], rows_of(to_lanes(*factors(16), target)), [other])
    all_of(6, pair_1.at[0]).wait_recv()
    twin_start = over_rank(pair_1[0] + pair_1[1]) * align_scale

    all_of(9, sums.at[pl.ds(0, 7)]).wait_recv()
    whole = jnp.sum(sums[...], axis=0)
    mixed = [whole[:16], whole[16:32]]
    norm = total(whole[32:33]) * (1.0 / rank)
    value = [rows_of(to_lanes(*factors(0), mixed)), rows_of(to_lanes(*factors(16), mixed)), squares(mixed)]
    share(7, pair_2, at["c"], jnp.concatenate(value, axis=0), [other])
    all_of(7, pair_2.at[0]).wait_recv()
    both = pair_2[0] + pair_2[1]
    product = over_rank(both[:16])
    alpha = norm / (total(both[16:17]) * scale + RIDGE * norm)
    start = jnp.concatenate([start, twin_start], axis=0)
    residual = start - alpha * (product * scale + RIDGE * start)

    line = line_of(residual)
    value = []
    for l in range(2):
        value.append(to_features(
            jnp.concatenate([factors(0)[0][l], factors(16)[0][l]], axis=1),
            jnp.concatenate([factors(0)[1][l], factors(16)[1][l]], axis=1),
            line,
        ))
    value.append(jnp.sum(residual * residual, axis=0, keepdims=True))
    value.append(jnp.sum(residual * start, axis=0, keepdims=True))
    share(10, last, two, jnp.concatenate(value, axis=0), next_twos)

    mine = lax.broadcasted_iota(jnp.int32, (16, LANES), 0) == plane_slot

    def own_row(value):
        return jnp.sum(jnp.where(mine, value, 0.0), axis=0, keepdims=True)

    start, residual, product = own_row(start), own_row(residual), own_row(product)
    weights = alpha * start
    left = [blocks[8 * l + plane_slot, :32] for l in range(2)]
    right = [blocks[8 * l + plane_slot, 32:] for l in range(2)]

    all_of(10, last.at[pl.ds(0, 3)]).wait_recv()
    whole = jnp.sum(last[...], axis=0)
    again = [whole[:16], whole[16:32]]
    norm_next = total(whole[32:33]) * (1.0 / rank)
    cross = total(whole[33:34]) * (1.0 / rank)
    beta = norm_next / norm
    again_row = to_lanes(left, right, again)
    square = squares([again[l] + beta * mixed[l] for l in range(2)])
    share(8, pair_3, at["c"], jnp.concatenate([again_row, square], axis=0), [other])
    direction = residual + beta * start
    length = norm_next + 2.0 * beta * cross + beta * beta * norm
    all_of(8, pair_3.at[0]).wait_recv()
    both = pair_3[0] + pair_3[1]
    product = over_rank(both)[:1] + beta * product
    image = product * scale + RIDGE * direction
    alpha = norm_next / (total(both[1:2]) * scale + RIDGE * length)
    out_ref[0:1] = weights + alpha * direction
    out_ref[1:2] = residual - alpha * image

    all_of(0, first.at[pl.ds(0, 7)]).wait_send()
    all_of(1, blocks.at[pl.ds(0, 15)]).wait_send()
    all_of(2, second.at[pl.ds(0, 15)]).wait_send()
    all_of(3, blocks.at[0]).wait_send()
    all_of(4, blocks.at[pl.ds(0, 15)]).wait_send()
    all_of(5, pair_0.at[0]).wait_send()
    all_of(6, pair_1.at[0]).wait_send()
    all_of(7, pair_2.at[0]).wait_send()
    all_of(8, pair_3.at[0]).wait_send()
    all_of(9, sums.at[pl.ds(0, 7)]).wait_send()
    all_of(10, last.at[pl.ds(0, 3)]).wait_send()


def per_device(left_factors, right_factors, left_proj, right_proj, val_ids):
    _, rows, rank, width = left_factors.shape
    left_proj = jnp.swapaxes(left_proj, 1, 2)
    right_proj = jnp.swapaxes(right_proj, 1, 2)
    ka, kb = left_proj.shape[1], right_proj.shape[1]
    val_count = val_ids.shape[0]
    total_features = ka * kb * lax.axis_size("feat")
    step = width // CHUNKS
    operands = (left_factors, right_factors, left_proj, right_proj, val_ids)
    out = pl.pallas_call(
        functools.partial(kernel, rows, rank, total_features, val_count),
        out_shape=jax.ShapeDtypeStruct((2, LANES), jnp.float32),
        in_specs=[pl.BlockSpec(memory_space=pltpu.HBM)] * 5,
        out_specs=pl.BlockSpec(memory_space=pltpu.VMEM),
        scratch_shapes=[
            pltpu.VMEM((CHUNKS, rows, rank, step), jnp.bfloat16),
            pltpu.VMEM((CHUNKS, rows, rank, step), jnp.bfloat16),
            pltpu.VMEM((ka, width), jnp.bfloat16),
            pltpu.VMEM((kb, width), jnp.bfloat16),
            pltpu.SMEM((val_count,), jnp.int32),
            pltpu.VMEM((32, ka + kb, LANES), jnp.bfloat16),
            pltpu.VMEM((8, 16, LANES), jnp.float32),
            pltpu.VMEM((16, 16, LANES), jnp.float32),
            pltpu.VMEM((8, 33, LANES), jnp.float32),
            pltpu.VMEM((4, 34, LANES), jnp.float32),
            pltpu.VMEM((2, 8, LANES), jnp.float32),
            pltpu.VMEM((2, 8, LANES), jnp.float32),
            pltpu.VMEM((2, 17, LANES), jnp.float32),
            pltpu.VMEM((2, 2, LANES), jnp.float32),
            pltpu.SemaphoreType.DMA((CHUNKS, 4)),
            pltpu.SemaphoreType.DMA,
            pltpu.SemaphoreType.DMA((11,)),
            pltpu.SemaphoreType.DMA((11,)),
        ],
        compiler_params=pltpu.CompilerParams(
            collective_id=0, has_side_effects=True, vmem_limit_bytes=32 * 2**20
        ),
        name="reweight",
    )(*(pltpu.with_memory_space_constraint(a, pltpu.HBM) for a in operands))
    return out[0, :rows], out[1, :rows]


def solution(mesh):
    return jax.shard_map(
        per_device,
        mesh=mesh,
        in_specs=(
            P("feat", "ex", None, None),
            P("feat", "ex", None, None),
            P("feat", None, None),
            P("feat", None, None),
            P(),
        ),
        out_specs=(P("ex"), P("ex")),
        check_vma=False,
    )
```

time: 37.9 us -> 36.8 us (0.971)
  local copies, waits for them, and re-layouts: 1.25 us -> 0.52 us
    squeeze x1, local copies, waits for them, and re-layouts: 1.25 us -> 0.52 us  [per_device(): return (out[0, :rows], out[1, :rows])]
where the time goes in v2:
time: 36.8 us; the launch traced here: 36.7 us
  Pallas kernels  35.6 us (97%)
  between operations  0.64 us (2%)
  local copies, waits for them, and re-layouts  0.52 us (1%)
    pallas_call x1, Pallas kernels, per_device(): pl.pallas_call(functools.partial(kernel, rows, rank, total_features, val_...  35.6 us

profile of v2, /device:TPU:1, one launch (start us, length us, event | category | flops | bytes accessed | tf_op | source)
XLA Modules:
  0.0 36.7 jit_solution(11532623749520318248)
XLA Ops:
  0.6 35.6 %reweight.1 = f32[2,128]{1,0:T(2,128)S(1)} custom-call(bf16[1,26,4,5120]{3,2,1,0:T(4,128)(2,1)} %lf_hbm.1, bf16[1,26,4,5120]{3,2,1,0:T(4,128)(2,1)} %rf_hbm.1, bf16[1,32,5120]{2,1,0:T(8,128)(2,1)} %bitcast.7, bf16[1,64,5120]{2,1,0:T(8,128)(2,1)} %bitcast.6, s32[256]{0:T(256)} %ids_hbm.1), custom_call_target="tpu_custom_call" | custom-call | tf_op jit(solution)/shard_map/reweight/pallas_call | solution.py:292
  36.2 0.5 %slice_bitcast_fusion = (f32[26]{0:T(128)}, f32[26]{0:T(128)}) fusion(f32[2,128]{1,0:T(2,128)S(1)} %reweight.1), kind=kLoop, calls=%fused_computation | loop fusion | bytes 416 | tf_op jit(solution)/shard_map/squeeze | solution.py:322

commit v3 on v2

--- a/solution.py
+++ b/solution.py
@@ -13,7 +13,7 @@
 NN = (((1,), (0,)), ((), ()))
 SIZE = dict(z=8, y=4, xh=2, xl=2, c=2)
 RIDGE = 0.5
-CHUNKS = 4
+CHUNKS = 2
 LANES = 128
 GROUP = 32
 
@@ -31,7 +31,7 @@
 def moved(at, **steps):
     new = dict(at)
     for axis, step in steps.items():
-        if not (isinstance(step, int) and step == 0):
+        if step:
             new[axis] = (at[axis] + step) % SIZE[axis]
     return new
 
@@ -90,6 +90,14 @@
     return jnp.sum(row, axis=1, keepdims=True)
 
 
+def thirds(value):
+    parts = []
+    for _ in range(3):
+        parts.append(value.astype(jnp.bfloat16).astype(jnp.float32))
+        value = value - parts[-1]
+    return parts + [jnp.zeros((10, LANES), jnp.float32)]
+
+
 def squares(values):
     return jnp.sum(values[0] * values[0] + values[1] * values[1], axis=0, keepdims=True)
 
@@ -97,7 +105,7 @@
 def kernel(
     rows, rank, total_features, val_count,
     lf_hbm, rf_hbm, lp_hbm, rp_hbm, ids_hbm, out_ref,
-    lf, rf, lp, rp, ids, blocks, first, second, sums, last, pair_0, pair_1, pair_2, pair_3,
+    lf, rf, lp, rp, ids, blocks, first, second, sums, pair_0, pair_1, pair_2,
     load_sem, ids_sem, send_sem, recv_sem,
 ):
     at = coordinates()
@@ -106,18 +114,20 @@
     used = rows * rank
     plane_slot = at["y"] * 2 + at["xh"]
     slot = at["xl"] * 8 + plane_slot
-    two = at["z"] // 2
-    sign = 2 * (at["z"] % 2) - 1
 
     along_z = [moved(at, z=d) for d in (4, 3, 5, 2, 6, 1, 7)]
-    next_twos = [moved(at, z=sign * d + 8) for d in (3, 2, 1)]
-    twin = moved(at, z=8 - sign)
     plane = [(y, xh, xl) for y in range(4) for xh in range(2) for xl in range(2) if y or xh or xl]
     plane = [moved(at, y=y, xh=xh, xl=xl) for y, xh, xl in sorted(plane, key=lambda o: -hops(*o))]
     other = moved(at, c=1)
     barrier = pltpu.get_barrier_semaphore()
-    for peer in along_z + plane + [other]:
-        pl.semaphore_signal(barrier, inc=1, device_id=device(peer), device_id_type=MESH)
+    order = along_z[:1] + plane[:1] + along_z[1:3] + plane[1:5]
+    rest = along_z[3:] + plane[5:] + [other]
+
+    def greet(peers):
+        for peer in peers:
+            pl.semaphore_signal(barrier, inc=1, device_id=device(peer), device_id_type=MESH)
+
+    greet(order)
 
     loads = []
     for i in range(CHUNKS):
@@ -133,6 +143,7 @@
         loads.append(group)
     load_ids = pltpu.make_async_copy(ids_hbm, ids, ids_sem)
     load_ids.start()
+    greet(rest)
 
     lane = lax.broadcasted_iota(jnp.int32, (8, LANES), 1) % GROUP
     own_id = jnp.where(lane < rows, (at["z"] * 8 + plane_slot) * rows + lane, -1)
@@ -156,8 +167,8 @@
     own = jnp.concatenate([left_part, right_part], axis=0).astype(jnp.bfloat16)
     source = lax.broadcasted_iota(jnp.int32, (used, LANES), 0)
     goal = lax.broadcasted_iota(jnp.int32, (used, LANES), 1)
-    order = jnp.where((source // rank == goal % GROUP) & (source % rank == goal // GROUP), 1.0, 0.0)
-    own = dot(own, order.astype(jnp.bfloat16), NN).astype(jnp.bfloat16)
+    place = jnp.where((source // rank == goal % GROUP) & (source % rank == goal // GROUP), 1.0, 0.0)
+    own = dot(own, place.astype(jnp.bfloat16), NN).astype(jnp.bfloat16)
     blocks[slot] = own
 
     def send(stage, source, goal, peers):
@@ -177,68 +188,50 @@
         buffer[index] = value
         send(stage, buffer.at[index], buffer.at[index], peers)
 
-    def factors(base):
-        left = [jnp.concatenate([blocks[base + 8 * l + b, :32] for b in range(8)], axis=1) for l in range(2)]
-        right = [jnp.concatenate([blocks[base + 8 * l + b, 32:] for b in range(8)], axis=1) for l in range(2)]
-        return left, right
-
     target = to_features(own[:32], own[32:], counts)
     pl.semaphore_wait(barrier, len(along_z) + len(plane) + 1)
-    share(0, first, at["z"], target, along_z)
+    share(0, first, at["z"], target.astype(first.dtype), along_z)
     send(1, blocks.at[slot], blocks.at[slot], plane)
-    send(3, blocks.at[slot], blocks.at[16 + slot], [twin])
     all_of(0, first.at[pl.ds(0, 7)]).wait_recv()
-    share(2, second, slot, jnp.sum(first[...], axis=0), plane)
-    all_of(3, blocks.at[16 + slot]).wait_recv()
-    send(4, blocks.at[16 + slot], blocks.at[16 + slot], plane)
+    share(2, second, slot, jnp.sum(first[...].astype(jnp.float32), axis=0).astype(second.dtype), plane)
     all_of(1, blocks.at[pl.ds(0, 15)]).wait_recv()
     all_of(2, second.at[pl.ds(0, 15)]).wait_recv()
-    target = [jnp.sum(second[pl.ds(8 * l, 8)], axis=0) for l in range(2)]
+    target = [jnp.sum(second[pl.ds(8 * l, 8)].astype(jnp.float32), axis=0) for l in range(2)]
+    left = [jnp.concatenate([blocks[8 * l + b, :32] for b in range(8)], axis=1) for l in range(2)]
+    right = [jnp.concatenate([blocks[8 * l + b, 32:] for b in range(8)], axis=1) for l in range(2)]
+
+    def send_features(index, rows, scalars):
+        line = line_of(rows)
+        value = [to_features(left[l], right[l], line) for l in range(2)]
+        value += thirds(jnp.concatenate([jnp.sum(s, axis=0, keepdims=True) for s in scalars], axis=0))
+        value = jnp.concatenate(value, axis=0).astype(jnp.bfloat16)
+        share(6 + index, sums.at[index], at["z"], value, along_z)
+
+    def take_features(index):
+        all_of(6 + index, sums.at[index, pl.ds(0, 7)]).wait_recv()
+        whole = jnp.sum(sums[index].astype(jnp.float32), axis=0)
+        scalars = total(whole[32:40] + whole[40:48]) * (1.0 / rank)
+        return [whole[:16], whole[16:32]], scalars[0:1] + scalars[2:3] + scalars[4:5], scalars[1:2] + scalars[3:4] + scalars[5:6]
 
     scale = 1.0 / (rank * total_features)
     align_scale = math.sqrt(val_count / total_features) / (val_count * rank)
 
-    share(5, pair_0, at["c"], rows_of(to_lanes(*factors(0), target)), [other])
-    all_of(5, pair_0.at[0]).wait_recv()
+    share(3, pair_0, at["c"], rows_of(to_lanes(left, right, target)), [other])
+    all_of(3, pair_0.at[0]).wait_recv()
     start = over_rank(pair_0[0] + pair_0[1]) * align_scale
-
-    left, right = factors(0)
-    line = line_of(start)
-    norm_row = jnp.sum(start * start, axis=0, keepdims=True)
-    value = jnp.concatenate([to_features(left[l], right[l], line) for l in range(2)] + [norm_row], axis=0)
-    share(9, sums, at["z"], value, along_z)
-
-    all_of(4, blocks.at[pl.ds(16, 15)]).wait_recv()
-    share(6, pair_1, at["c"], rows_of(to_lanes(*factors(16), target)), [other])
-    all_of(6, pair_1.at[0]).wait_recv()
-    twin_start = over_rank(pair_1[0] + pair_1[1]) * align_scale
-
-    all_of(9, sums.at[pl.ds(0, 7)]).wait_recv()
-    whole = jnp.sum(sums[...], axis=0)
-    mixed = [whole[:16], whole[16:32]]
-    norm = total(whole[32:33]) * (1.0 / rank)
-    value = [rows_of(to_lanes(*factors(0), mixed)), rows_of(to_lanes(*factors(16), mixed)), squares(mixed)]
-    share(7, pair_2, at["c"], jnp.concatenate(value, axis=0), [other])
-    all_of(7, pair_2.at[0]).wait_recv()
-    both = pair_2[0] + pair_2[1]
-    product = over_rank(both[:16])
-    alpha = norm / (total(both[16:17]) * scale + RIDGE * norm)
-    start = jnp.concatenate([start, twin_start], axis=0)
+    send_features(0, start, [start * start, start])
+    mixed, norm, _ = take_features(0)
+
+    value = jnp.concatenate([rows_of(to_lanes(left, right, mixed)), squares(mixed)], axis=0)
+    share(4, pair_1, at["c"], value, [other])
+    all_of(4, pair_1.at[0]).wait_recv()
+    both = pair_1[0] + pair_1[1]
+    product = over_rank(both[:8])
+    alpha = norm / (total(both[8:9]) * scale + RIDGE * norm)
     residual = start - alpha * (product * scale + RIDGE * start)
-
-    line = line_of(residual)
-    value = []
-    for l in range(2):
-        value.append(to_features(
-            jnp.concatenate([factors(0)[0][l], factors(16)[0][l]], axis=1),
-            jnp.concatenate([factors(0)[1][l], factors(16)[1][l]], axis=1),
-            line,
-        ))
-    value.append(jnp.sum(residual * residual, axis=0, keepdims=True))
-    value.append(jnp.sum(residual * start, axis=0, keepdims=True))
-    share(10, last, two, jnp.concatenate(value, axis=0), next_twos)
-
-    mine = lax.broadcasted_iota(jnp.int32, (16, LANES), 0) == plane_slot
+    send_features(1, residual, [residual * residual, residual * start])
+
+    mine = lax.broadcasted_iota(jnp.int32, (8, LANES), 0) == plane_slot
 
     def own_row(value):
         return jnp.sum(jnp.where(mine, value, 0.0), axis=0, keepdims=True)
@@ -248,19 +241,15 @@
     left = [blocks[8 * l + plane_slot, :32] for l in range(2)]
     right = [blocks[8 * l + plane_slot, 32:] for l in range(2)]
 
-    all_of(10, last.at[pl.ds(0, 3)]).wait_recv()
-    whole = jnp.sum(last[...], axis=0)
-    again = [whole[:16], whole[16:32]]
-    norm_next = total(whole[32:33]) * (1.0 / rank)
-    cross = total(whole[33:34]) * (1.0 / rank)
+    again, norm_next, cross = take_features(1)
     beta = norm_next / norm
     again_row = to_lanes(left, right, again)
     square = squares([again[l] + beta * mixed[l] for l in range(2)])
-    share(8, pair_3, at["c"], jnp.concatenate([again_row, square], axis=0), [other])
+    share(5, pair_2, at["c"], jnp.concatenate([again_row, square], axis=0), [other])
     direction = residual + beta * start
     length = norm_next + 2.0 * beta * cross + beta * beta * norm
-    all_of(8, pair_3.at[0]).wait_recv()
-    both = pair_3[0] + pair_3[1]
+    all_of(5, pair_2.at[0]).wait_recv()
+    both = pair_2[0] + pair_2[1]
     product = over_rank(both)[:1] + beta * product
     image = product * scale + RIDGE * direction
     alpha = norm_next / (total(both[1:2]) * scale + RIDGE * length)
@@ -270,14 +259,10 @@
     all_of(0, first.at[pl.ds(0, 7)]).wait_send()
     all_of(1, blocks.at[pl.ds(0, 15)]).wait_send()
     all_of(2, second.at[pl.ds(0, 15)]).wait_send()
-    all_of(3, blocks.at[0]).wait_send()
-    all_of(4, blocks.at[pl.ds(0, 15)]).wait_send()
-    all_of(5, pair_0.at[0]).wait_send()
-    all_of(6, pair_1.at[0]).wait_send()
-    all_of(7, pair_2.at[0]).wait_send()
-    all_of(8, pair_3.at[0]).wait_send()
-    all_of(9, sums.at[pl.ds(0, 7)]).wait_send()
-    all_of(10, last.at[pl.ds(0, 3)]).wait_send()
+    for i, pair in enumerate((pair_0, pair_1, pair_2)):
+        all_of(3 + i, pair.at[0]).wait_send()
+    for i in range(2):
+        all_of(6 + i, sums.at[i, pl.ds(0, 7)]).wait_send()
 
 
 def per_device(left_factors, right_factors, left_proj, right_proj, val_ids):
@@ -300,19 +285,17 @@
             pltpu.VMEM((ka, width), jnp.bfloat16),
             pltpu.VMEM((kb, width), jnp.bfloat16),
             pltpu.SMEM((val_count,), jnp.int32),
-            pltpu.VMEM((32, ka + kb, LANES), jnp.bfloat16),
-            pltpu.VMEM((8, 16, LANES), jnp.float32),
-            pltpu.VMEM((16, 16, LANES), jnp.float32),
-            pltpu.VMEM((8, 33, LANES), jnp.float32),
-            pltpu.VMEM((4, 34, LANES), jnp.float32),
+            pltpu.VMEM((16, ka + kb, LANES), jnp.bfloat16),
+            pltpu.VMEM((8, 16, LANES), jnp.bfloat16),
+            pltpu.VMEM((16, 16, LANES), jnp.bfloat16),
+            pltpu.VMEM((2, 8, 48, LANES), jnp.bfloat16),
             pltpu.VMEM((2, 8, LANES), jnp.float32),
-            pltpu.VMEM((2, 8, LANES), jnp.float32),
-            pltpu.VMEM((2, 17, LANES), jnp.float32),
+            pltpu.VMEM((2, 9, LANES), jnp.float32),
             pltpu.VMEM((2, 2, LANES), jnp.float32),
             pltpu.SemaphoreType.DMA((CHUNKS, 4)),
             pltpu.SemaphoreType.DMA,
-            pltpu.SemaphoreType.DMA((11,)),
-            pltpu.SemaphoreType.DMA((11,)),
+            pltpu.SemaphoreType.DMA((8,)),
+            pltpu.SemaphoreType.DMA((8,)),
         ],
         compiler_params=pltpu.CompilerParams(
             collective_id=0, has_side_effects=True, vmem_limit_bytes=32 * 2**20

time: 36.8 us -> 35.6 us (0.967)
  Pallas kernels: 35.6 us -> 34.3 us
    pallas_call x1, Pallas kernels: 35.6 us -> 34.3 us  [per_device(): pl.pallas_call(functools.partial(kernel, rows, rank, total_features, val_...]
where the time goes in v3:
time: 35.6 us; the launch traced here: 35.5 us
  Pallas kernels  34.3 us (96%)
  between operations  0.64 us (2%)
  local copies, waits for them, and re-layouts  0.52 us (1%)
    pallas_call x1, Pallas kernels, per_device(): pl.pallas_call(functools.partial(kernel, rows, rank, total_features, val_...  34.3 us

profile of v3, /device:TPU:1, one launch (start us, length us, event | category | flops | bytes accessed | tf_op | source)
XLA Modules:
  0.0 35.5 jit_solution(16831932944895187095)
XLA Ops:
  0.6 34.3 %reweight.1 = f32[2,128]{1,0:T(2,128)S(1)} custom-call(bf16[1,26,4,5120]{3,2,1,0:T(4,128)(2,1)} %lf_hbm.1, bf16[1,26,4,5120]{3,2,1,0:T(4,128)(2,1)} %rf_hbm.1, bf16[1,32,5120]{2,1,0:T(8,128)(2,1)} %bitcast.7, bf16[1,64,5120]{2,1,0:T(8,128)(2,1)} %bitcast.6, s32[256]{0:T(256)} %ids_hbm.1), custom_call_target="tpu_custom_call" | custom-call | tf_op jit(solution)/shard_map/reweight/pallas_call | solution.py:277
  35.0 0.5 %slice_bitcast_fusion = (f32[26]{0:T(128)}, f32[26]{0:T(128)}) fusion(f32[2,128]{1,0:T(2,128)S(1)} %reweight.1), kind=kLoop, calls=%fused_computation | loop fusion | bytes 416 | tf_op jit(solution)/shard_map/squeeze | solution.py:305

commit v4 on v3

--- a/solution.py
+++ b/solution.py
@@ -64,21 +64,13 @@
     return pack(sums[:32] + sums[32:])
 
 
-def to_lanes(left, right, values):
+def to_lanes(left, right, values, ranks=lambda term: term):
     total = None
     for l in range(2):
         mixed = dot(split(unpack(values[l])), right[l], NN)
-        term = (mixed[:32] + mixed[32:]) * left[l].astype(jnp.float32)
+        term = ranks((mixed[:32] + mixed[32:]) * left[l].astype(jnp.float32))
         total = term if total is None else total + term
     return jnp.sum(total, axis=0, keepdims=True)
-
-
-def rows_of(line):
-    return jnp.concatenate([line[:, i:i + LANES] for i in range(0, line.shape[1], LANES)], axis=0)
-
-
-def line_of(rows):
-    return jnp.concatenate([rows[i:i + 1] for i in range(rows.shape[0])], axis=1)
 
 
 def over_rank(rows):
@@ -90,22 +82,23 @@
     return jnp.sum(row, axis=1, keepdims=True)
 
 
-def thirds(value):
-    parts = []
-    for _ in range(3):
-        parts.append(value.astype(jnp.bfloat16).astype(jnp.float32))
-        value = value - parts[-1]
-    return parts + [jnp.zeros((10, LANES), jnp.float32)]
-
-
-def squares(values):
-    return jnp.sum(values[0] * values[0] + values[1] * values[1], axis=0, keepdims=True)
+def products(a, b):
+    return jnp.sum(a[0] * b[0] + a[1] * b[1], axis=0, keepdims=True)
+
+
+def halves(line):
+    return line[:, :LANES] + line[:, LANES:]
+
+
+def ranks_added(line):
+    n = line.shape[1] // 4
+    return (line[:, :n] + line[:, n:2 * n]) + (line[:, 2 * n:3 * n] + line[:, 3 * n:])
 
 
 def kernel(
     rows, rank, total_features, val_count,
     lf_hbm, rf_hbm, lp_hbm, rp_hbm, ids_hbm, out_ref,
-    lf, rf, lp, rp, ids, blocks, first, second, sums, pair_0, pair_1, pair_2,
+    lf, rf, lp, rp, ids, blocks, wide, first, second, sums, norms, pair_0, pair_1, pair_2,
     load_sem, ids_sem, send_sem, recv_sem,
 ):
     at = coordinates()
@@ -195,64 +188,85 @@
     all_of(0, first.at[pl.ds(0, 7)]).wait_recv()
     share(2, second, slot, jnp.sum(first[...].astype(jnp.float32), axis=0).astype(second.dtype), plane)
     all_of(1, blocks.at[pl.ds(0, 15)]).wait_recv()
+    segment = lax.broadcasted_iota(jnp.int32, (96, LANES), 1) // GROUP
+    for l in range(2):
+        for h in range(2):
+            four = [blocks[8 * l + 4 * h + j].astype(jnp.float32) for j in range(4)]
+            for r in range(4):
+                moves = [pltpu.roll(four[j], GROUP * ((j - r) % 4), 1) if j != r else four[j] for j in range(4)]
+                value = jnp.where(
+                    segment < 2, jnp.where(segment == 0, moves[0], moves[1]),
+                    jnp.where(segment == 2, moves[2], moves[3]),
+                )
+                lanes = slice(256 * r + LANES * h, 256 * r + LANES * h + LANES)
+                wide[l, :, lanes] = value.astype(jnp.bfloat16)
+    left = [wide[l, :32] for l in range(2)]
+    right = [wide[l, 32:] for l in range(2)]
     all_of(2, second.at[pl.ds(0, 15)]).wait_recv()
     target = [jnp.sum(second[pl.ds(8 * l, 8)].astype(jnp.float32), axis=0) for l in range(2)]
-    left = [jnp.concatenate([blocks[8 * l + b, :32] for b in range(8)], axis=1) for l in range(2)]
-    right = [jnp.concatenate([blocks[8 * l + b, 32:] for b in range(8)], axis=1) for l in range(2)]
-
-    def send_features(index, rows, scalars):
-        line = line_of(rows)
-        value = [to_features(left[l], right[l], line) for l in range(2)]
-        value += thirds(jnp.concatenate([jnp.sum(s, axis=0, keepdims=True) for s in scalars], axis=0))
-        value = jnp.concatenate(value, axis=0).astype(jnp.bfloat16)
-        share(6 + index, sums.at[index], at["z"], value, along_z)
+
+    def all_ranks(line):
+        line = jnp.concatenate([line] * 4, axis=1)
+        return [to_features(left[l], right[l], line) for l in range(2)]
+
+    def send_features(index, values, scalars):
+        share(6 + index, sums.at[index], at["z"], jnp.concatenate(values, axis=0).astype(jnp.bfloat16), along_z)
+        share(8 + index, norms.at[index], at["z"], jnp.concatenate([halves(s) for s in scalars], axis=1), along_z)
 
     def take_features(index):
         all_of(6 + index, sums.at[index, pl.ds(0, 7)]).wait_recv()
         whole = jnp.sum(sums[index].astype(jnp.float32), axis=0)
-        scalars = total(whole[32:40] + whole[40:48]) * (1.0 / rank)
-        return [whole[:16], whole[16:32]], scalars[0:1] + scalars[2:3] + scalars[4:5], scalars[1:2] + scalars[3:4] + scalars[5:6]
+        return [whole[:16], whole[16:]]
+
+    def take_norms(index):
+        all_of(8 + index, norms.at[index, pl.ds(0, 7)]).wait_recv()
+        whole = jnp.sum(norms[index], axis=0)
+        return total(whole[:, :LANES]), total(whole[:, LANES:])
 
     scale = 1.0 / (rank * total_features)
     align_scale = math.sqrt(val_count / total_features) / (val_count * rank)
 
-    share(3, pair_0, at["c"], rows_of(to_lanes(left, right, target)), [other])
+    share(3, pair_0, at["c"], to_lanes(left, right, target, ranks_added), [other])
     all_of(3, pair_0.at[0]).wait_recv()
-    start = over_rank(pair_0[0] + pair_0[1]) * align_scale
-    send_features(0, start, [start * start, start])
-    mixed, norm, _ = take_features(0)
-
-    value = jnp.concatenate([rows_of(to_lanes(left, right, mixed)), squares(mixed)], axis=0)
-    share(4, pair_1, at["c"], value, [other])
+    start = (pair_0[0] + pair_0[1]) * align_scale
+    start_parts = all_ranks(start)
+    send_features(0, start_parts, [start * start, start])
+    mixed = take_features(0)
+
+    value = [to_lanes(left, right, mixed, ranks_added), products(mixed, mixed)]
+    share(4, pair_1, at["c"], jnp.concatenate(value, axis=1), [other])
+    norm, _ = take_norms(0)
     all_of(4, pair_1.at[0]).wait_recv()
     both = pair_1[0] + pair_1[1]
-    product = over_rank(both[:8])
-    alpha = norm / (total(both[8:9]) * scale + RIDGE * norm)
+    product = both[:, :256]
+    alpha = norm / (total(both[:, 256:]) * scale + RIDGE * norm)
     residual = start - alpha * (product * scale + RIDGE * start)
-    send_features(1, residual, [residual * residual, residual * start])
-
-    mine = lax.broadcasted_iota(jnp.int32, (8, LANES), 0) == plane_slot
+    parts = all_ranks(residual)
+    send_features(1, parts, [residual * residual, residual * start])
+
+    mine = lax.broadcasted_iota(jnp.int32, (1, 256), 1) // GROUP == plane_slot
 
     def own_row(value):
-        return jnp.sum(jnp.where(mine, value, 0.0), axis=0, keepdims=True)
-
+        return over_rank(halves(jnp.where(mine, value, 0.0)))
+
+    mixed_square = total(both[:, 256:])
     start, residual, product = own_row(start), own_row(residual), own_row(product)
     weights = alpha * start
     left = [blocks[8 * l + plane_slot, :32] for l in range(2)]
     right = [blocks[8 * l + plane_slot, 32:] for l in range(2)]
 
-    again, norm_next, cross = take_features(1)
+    again = take_features(1)
+    value = [to_lanes(left, right, again), products(again, again), products(again, mixed)]
+    share(5, pair_2, at["c"], jnp.concatenate(value, axis=1), [other])
+    norm_next, cross = take_norms(1)
     beta = norm_next / norm
-    again_row = to_lanes(left, right, again)
-    square = squares([again[l] + beta * mixed[l] for l in range(2)])
-    share(5, pair_2, at["c"], jnp.concatenate([again_row, square], axis=0), [other])
     direction = residual + beta * start
     length = norm_next + 2.0 * beta * cross + beta * beta * norm
     all_of(5, pair_2.at[0]).wait_recv()
     both = pair_2[0] + pair_2[1]
-    product = over_rank(both)[:1] + beta * product
-    image = product * scale + RIDGE * direction
-    alpha = norm_next / (total(both[1:2]) * scale + RIDGE * length)
+    square = total(both[:, LANES:2 * LANES]) + 2.0 * beta * total(both[:, 2 * LANES:]) + beta * beta * mixed_square
+    alpha = norm_next / (square * scale + RIDGE * length)
+    image = (over_rank(both[:, :LANES]) + beta * product) * scale + RIDGE * direction
     out_ref[0:1] = weights + alpha * direction
     out_ref[1:2] = residual - alpha * image
 
@@ -263,6 +277,7 @@
         all_of(3 + i, pair.at[0]).wait_send()
     for i in range(2):
         all_of(6 + i, sums.at[i, pl.ds(0, 7)]).wait_send()
+        all_of(8 + i, norms.at[i, pl.ds(0, 7)]).wait_send()
 
 
 def per_device(left_factors, right_factors, left_proj, right_proj, val_ids):
@@ -286,16 +301,18 @@
             pltpu.VMEM((kb, width), jnp.bfloat16),
             pltpu.SMEM((val_count,), jnp.int32),
             pltpu.VMEM((16, ka + kb, LANES), jnp.bfloat16),
+            pltpu.VMEM((2, ka + kb, 8 * LANES), jnp.bfloat16),
             pltpu.VMEM((8, 16, LANES), jnp.bfloat16),
             pltpu.VMEM((16, 16, LANES), jnp.bfloat16),
-            pltpu.VMEM((2, 8, 48, LANES), jnp.bfloat16),
-            pltpu.VMEM((2, 8, LANES), jnp.float32),
-            pltpu.VMEM((2, 9, LANES), jnp.float32),
-            pltpu.VMEM((2, 2, LANES), jnp.float32),
+            pltpu.VMEM((2, 8, 32, LANES), jnp.bfloat16),
+            pltpu.VMEM((2, 8, 1, 2 * LANES), jnp.float32),
+            pltpu.VMEM((2, 1, 2 * LANES), jnp.float32),
+            pltpu.VMEM((2, 1, 3 * LANES), jnp.float32),
+            pltpu.VMEM((2, 1, 3 * LANES), jnp.float32),
             pltpu.SemaphoreType.DMA((CHUNKS, 4)),
             pltpu.SemaphoreType.DMA,
-            pltpu.SemaphoreType.DMA((8,)),
-            pltpu.SemaphoreType.DMA((8,)),
+            pltpu.SemaphoreType.DMA((10,)),
+            pltpu.SemaphoreType.DMA((10,)),
         ],
         compiler_params=pltpu.CompilerParams(
             collective_id=0, has_side_effects=True, vmem_limit_bytes=32 * 2**20

time: 35.6 us -> 34.7 us (0.975)
  Pallas kernels: 34.3 us -> 33.4 us
    pallas_call x1, Pallas kernels: 34.3 us -> 33.4 us  [per_device(): pl.pallas_call(functools.partial(kernel, rows, rank, total_features, val_...]
where the time goes in v4:
time: 34.7 us; the launch traced here: 34.6 us
  Pallas kernels  33.4 us (96%)
  between operations  0.64 us (2%)
  local copies, waits for them, and re-layouts  0.52 us (1%)
    pallas_call x1, Pallas kernels, per_device(): pl.pallas_call(functools.partial(kernel, rows, rank, total_features, val_...  33.4 us

profile of v4, /device:TPU:1, one launch (start us, length us, event | category | flops | bytes accessed | tf_op | source)
XLA Modules:
  0.0 34.6 jit_solution(15213371369695295537)
XLA Ops:
  0.6 33.4 %reweight.1 = f32[2,128]{1,0:T(2,128)S(1)} custom-call(bf16[1,26,4,5120]{3,2,1,0:T(4,128)(2,1)} %lf_hbm.1, bf16[1,26,4,5120]{3,2,1,0:T(4,128)(2,1)} %rf_hbm.1, bf16[1,32,5120]{2,1,0:T(8,128)(2,1)} %bitcast.7, bf16[1,64,5120]{2,1,0:T(8,128)(2,1)} %bitcast.6, s32[256]{0:T(256)} %ids_hbm.1), custom_call_target="tpu_custom_call" | custom-call | tf_op jit(solution)/shard_map/reweight/pallas_call | solution.py:292
  34.1 0.5 %slice_bitcast_fusion = (f32[26]{0:T(128)}, f32[26]{0:T(128)}) fusion(f32[2,128]{1,0:T(2,128)S(1)} %reweight.1), kind=kLoop, calls=%fused_computation | loop fusion | bytes 416 | tf_op jit(solution)/shard_map/squeeze | solution.py:322

commit v5 on v4

--- a/solution.py
+++ b/solution.py
@@ -31,7 +31,7 @@
 def moved(at, **steps):
     new = dict(at)
     for axis, step in steps.items():
-        if step:
+        if not isinstance(step, int) or step:
             new[axis] = (at[axis] + step) % SIZE[axis]
     return new
 
@@ -106,15 +106,21 @@
     step = width // CHUNKS
     used = rows * rank
     plane_slot = at["y"] * 2 + at["xh"]
-    slot = at["xl"] * 8 + plane_slot
+    near = at["z"] % 2
+    own_slot = (at["z"] // 2) * 2 + at["xh"]
+    slot = at["xl"] * 8 + own_slot
+    group_slot = at["y"] * 2 + near
 
     along_z = [moved(at, z=d) for d in (4, 3, 5, 2, 6, 1, 7)]
     plane = [(y, xh, xl) for y in range(4) for xh in range(2) for xl in range(2) if y or xh or xl]
     plane = [moved(at, y=y, xh=xh, xl=xl) for y, xh, xl in sorted(plane, key=lambda o: -hops(*o))]
     other = moved(at, c=1)
+    along_x = [moved(at, xh=xh, xl=xl) for xh, xl in ((1, 0), (0, 1), (1, 1))]
+    twins = [moved(at, y=y, z=1 - 2 * near) for y in (2, 1, 3, 0)]
+    sharers = [twins[0], moved(at, y=2)] + twins[1:3] + [moved(at, y=1), moved(at, y=3), twins[3]]
     barrier = pltpu.get_barrier_semaphore()
-    order = along_z[:1] + plane[:1] + along_z[1:3] + plane[1:5]
-    rest = along_z[3:] + plane[5:] + [other]
+    order = along_z[:1] + plane[:1] + along_z[1:3] + plane[1:5] + twins[:1]
+    rest = along_z[3:] + plane[5:] + twins[1:3] + [other]
 
     def greet(peers):
         for peer in peers:
@@ -182,12 +188,27 @@
         send(stage, buffer.at[index], buffer.at[index], peers)
 
     target = to_features(own[:32], own[32:], counts)
-    pl.semaphore_wait(barrier, len(along_z) + len(plane) + 1)
-    share(0, first, at["z"], target.astype(first.dtype), along_z)
-    send(1, blocks.at[slot], blocks.at[slot], plane)
-    all_of(0, first.at[pl.ds(0, 7)]).wait_recv()
-    share(2, second, slot, jnp.sum(first[...].astype(jnp.float32), axis=0).astype(second.dtype), plane)
-    all_of(1, blocks.at[pl.ds(0, 15)]).wait_recv()
+    pl.semaphore_wait(barrier, len(order) + len(rest))
+    index = at["xl"] * 8 + plane_slot
+    first[index] = target.astype(first.dtype)
+    send(0, first.at[index], first.at[index], plane[:5])
+    for d in (2, 1, 3):
+        send(9 + d, blocks.at[slot], blocks.at[slot], [moved(at, z=2 * d)])
+    send(0, first.at[index], first.at[index], plane[5:])
+    send(1, blocks.at[slot], blocks.at[slot], along_x)
+
+    def forward(d):
+        come = at["xl"] * 8 + ((at["z"] // 2 + 4 - d) % 4) * 2 + at["xh"]
+        all_of(9 + d, blocks.at[come]).wait_recv()
+        send(1, blocks.at[come], blocks.at[come], along_x)
+
+    forward(1)
+    forward(3)
+    all_of(0, first.at[pl.ds(0, 15)]).wait_recv()
+    target = [jnp.sum(first[pl.ds(8 * l, 8)].astype(jnp.float32), axis=0) for l in range(2)]
+    share(2, second, at["z"], jnp.concatenate(target, axis=0).astype(second.dtype), along_z)
+    forward(2)
+    all_of(1, blocks.at[pl.ds(0, 12)]).wait_recv()
     segment = lax.broadcasted_iota(jnp.int32, (96, LANES), 1) // GROUP
     for l in range(2):
         for h in range(2):
@@ -202,16 +223,17 @@
                 wide[l, :, lanes] = value.astype(jnp.bfloat16)
     left = [wide[l, :32] for l in range(2)]
     right = [wide[l, 32:] for l in range(2)]
-    all_of(2, second.at[pl.ds(0, 15)]).wait_recv()
-    target = [jnp.sum(second[pl.ds(8 * l, 8)].astype(jnp.float32), axis=0) for l in range(2)]
+    all_of(2, second.at[pl.ds(0, 7)]).wait_recv()
+    target = jnp.sum(second[...].astype(jnp.float32), axis=0)
+    target = [target[:16], target[16:]]
 
     def all_ranks(line):
         line = jnp.concatenate([line] * 4, axis=1)
         return [to_features(left[l], right[l], line) for l in range(2)]
 
     def send_features(index, values, scalars):
-        share(6 + index, sums.at[index], at["z"], jnp.concatenate(values, axis=0).astype(jnp.bfloat16), along_z)
-        share(8 + index, norms.at[index], at["z"], jnp.concatenate([halves(s) for s in scalars], axis=1), along_z)
+        share(6 + index, sums.at[index], group_slot, jnp.concatenate(values, axis=0).astype(jnp.bfloat16), sharers)
+        share(8 + index, norms.at[index], group_slot, jnp.concatenate([halves(s) for s in scalars], axis=1), sharers)
 
     def take_features(index):
         all_of(6 + index, sums.at[index, pl.ds(0, 7)]).wait_recv()
@@ -244,7 +266,7 @@
     parts = all_ranks(residual)
     send_features(1, parts, [residual * residual, residual * start])
 
-    mine = lax.broadcasted_iota(jnp.int32, (1, 256), 1) // GROUP == plane_slot
+    mine = lax.broadcasted_iota(jnp.int32, (1, 256), 1) // GROUP == own_slot
 
     def own_row(value):
         return over_rank(halves(jnp.where(mine, value, 0.0)))
@@ -252,8 +274,8 @@
     mixed_square = total(both[:, 256:])
     start, residual, product = own_row(start), own_row(residual), own_row(product)
     weights = alpha * start
-    left = [blocks[8 * l + plane_slot, :32] for l in range(2)]
-    right = [blocks[8 * l + plane_slot, 32:] for l in range(2)]
+    left = [blocks[8 * l + own_slot, :32] for l in range(2)]
+    right = [blocks[8 * l + own_slot, 32:] for l in range(2)]
 
     again = take_features(1)
     value = [to_lanes(left, right, again), products(again, again), products(again, mixed)]
@@ -270,9 +292,11 @@
     out_ref[0:1] = weights + alpha * direction
     out_ref[1:2] = residual - alpha * image
 
-    all_of(0, first.at[pl.ds(0, 7)]).wait_send()
-    all_of(1, blocks.at[pl.ds(0, 15)]).wait_send()
-    all_of(2, second.at[pl.ds(0, 15)]).wait_send()
+    all_of(0, first.at[pl.ds(0, 15)]).wait_send()
+    all_of(1, blocks.at[pl.ds(0, 12)]).wait_send()
+    for d in (1, 2, 3):
+        all_of(9 + d, blocks.at[0]).wait_send()
+    all_of(2, second.at[pl.ds(0, 7)]).wait_send()
     for i, pair in enumerate((pair_0, pair_1, pair_2)):
         all_of(3 + i, pair.at[0]).wait_send()
     for i in range(2):
@@ -302,8 +326,8 @@
             pltpu.SMEM((val_count,), jnp.int32),
             pltpu.VMEM((16, ka + kb, LANES), jnp.bfloat16),
             pltpu.VMEM((2, ka + kb, 8 * LANES), jnp.bfloat16),
-            pltpu.VMEM((8, 16, LANES), jnp.bfloat16),
             pltpu.VMEM((16, 16, LANES), jnp.bfloat16),
+            pltpu.VMEM((8, 32, LANES), jnp.bfloat16),
             pltpu.VMEM((2, 8, 32, LANES), jnp.bfloat16),
             pltpu.VMEM((2, 8, 1, 2 * LANES), jnp.float32),
             pltpu.VMEM((2, 1, 2 * LANES), jnp.float32),
@@ -311,8 +335,8 @@
             pltpu.VMEM((2, 1, 3 * LANES), jnp.float32),
             pltpu.SemaphoreType.DMA((CHUNKS, 4)),
             pltpu.SemaphoreType.DMA,
-            pltpu.SemaphoreType.DMA((10,)),
-            pltpu.SemaphoreType.DMA((10,)),
+            pltpu.SemaphoreType.DMA((13,)),
+            pltpu.SemaphoreType.DMA((13,)),
         ],
         compiler_params=pltpu.CompilerParams(
             collective_id=0, has_side_effects=True, vmem_limit_bytes=32 * 2**20

time: 34.7 us -> 33.6 us (0.968)
  Pallas kernels: 33.4 us -> 32.3 us
    pallas_call x1, Pallas kernels: 33.4 us -> 32.3 us  [per_device(): pl.pallas_call(functools.partial(kernel, rows, rank, total_features, val_...]
where the time goes in v5:
time: 33.6 us; the launch traced here: 33.5 us
  Pallas kernels  32.3 us (96%)
  between operations  0.64 us (2%)
  local copies, waits for them, and re-layouts  0.52 us (2%)
    pallas_call x1, Pallas kernels, per_device(): pl.pallas_call(functools.partial(kernel, rows, rank, total_features, val_...  32.3 us

profile of v5, /device:TPU:1, one launch (start us, length us, event | category | flops | bytes accessed | tf_op | source)
XLA Modules:
  0.0 33.5 jit_solution(14603675663637559075)
XLA Ops:
  0.6 32.3 %reweight.1 = f32[2,128]{1,0:T(2,128)S(1)} custom-call(bf16[1,26,4,5120]{3,2,1,0:T(4,128)(2,1)} %lf_hbm.1, bf16[1,26,4,5120]{3,2,1,0:T(4,128)(2,1)} %rf_hbm.1, bf16[1,32,5120]{2,1,0:T(8,128)(2,1)} %bitcast.7, bf16[1,64,5120]{2,1,0:T(8,128)(2,1)} %bitcast.6, s32[256]{0:T(256)} %ids_hbm.1), custom_call_target="tpu_custom_call" | custom-call | tf_op jit(solution)/shard_map/reweight/pallas_call | solution.py:316
  33.0 0.5 %slice_bitcast_fusion = (f32[26]{0:T(128)}, f32[26]{0:T(128)}) fusion(f32[2,128]{1,0:T(2,128)S(1)} %reweight.1), kind=kLoop, calls=%fused_computation | loop fusion | bytes 416 | tf_op jit(solution)/shard_map/squeeze | solution.py:346

commit v6 on v5

--- a/solution.py
+++ b/solution.py
@@ -13,7 +13,7 @@
 NN = (((1,), (0,)), ((), ()))
 SIZE = dict(z=8, y=4, xh=2, xl=2, c=2)
 RIDGE = 0.5
-CHUNKS = 2
+CHUNKS = 4
 LANES = 128
 GROUP = 32
 
@@ -107,7 +107,7 @@
     used = rows * rank
     plane_slot = at["y"] * 2 + at["xh"]
     near = at["z"] % 2
-    own_slot = (at["z"] // 2) * 2 + at["xh"]
+    own_slot = at["xh"]
     slot = at["xl"] * 8 + own_slot
     group_slot = at["y"] * 2 + near
 
@@ -189,29 +189,22 @@
 
     target = to_features(own[:32], own[32:], counts)
     pl.semaphore_wait(barrier, len(order) + len(rest))
+    place_of = {1: 1, 3: 2, 2: 3}
     index = at["xl"] * 8 + plane_slot
     first[index] = target.astype(first.dtype)
     send(0, first.at[index], first.at[index], plane[:5])
     for d in (2, 1, 3):
-        send(9 + d, blocks.at[slot], blocks.at[slot], [moved(at, z=2 * d)])
+        send(9 + d, blocks.at[slot], blocks.at[slot + 2 * place_of[d]], [moved(at, z=2 * d)])
     send(0, first.at[index], first.at[index], plane[5:])
     send(1, blocks.at[slot], blocks.at[slot], along_x)
 
     def forward(d):
-        come = at["xl"] * 8 + ((at["z"] // 2 + 4 - d) % 4) * 2 + at["xh"]
+        come = slot + 2 * place_of[d]
         all_of(9 + d, blocks.at[come]).wait_recv()
-        send(1, blocks.at[come], blocks.at[come], along_x)
-
-    forward(1)
-    forward(3)
-    all_of(0, first.at[pl.ds(0, 15)]).wait_recv()
-    target = [jnp.sum(first[pl.ds(8 * l, 8)].astype(jnp.float32), axis=0) for l in range(2)]
-    share(2, second, at["z"], jnp.concatenate(target, axis=0).astype(second.dtype), along_z)
-    forward(2)
-    all_of(1, blocks.at[pl.ds(0, 12)]).wait_recv()
-    segment = lax.broadcasted_iota(jnp.int32, (96, LANES), 1) // GROUP
-    for l in range(2):
-        for h in range(2):
+        send(1 if d == 1 else 13, blocks.at[come], blocks.at[come], along_x)
+
+    def lay_out(h):
+        for l in range(2):
             four = [blocks[8 * l + 4 * h + j].astype(jnp.float32) for j in range(4)]
             for r in range(4):
                 moves = [pltpu.roll(four[j], GROUP * ((j - r) % 4), 1) if j != r else four[j] for j in range(4)]
@@ -221,6 +214,18 @@
                 )
                 lanes = slice(256 * r + LANES * h, 256 * r + LANES * h + LANES)
                 wide[l, :, lanes] = value.astype(jnp.bfloat16)
+
+    segment = lax.broadcasted_iota(jnp.int32, (96, LANES), 1) // GROUP
+    forward(1)
+    forward(3)
+    all_of(0, first.at[pl.ds(0, 15)]).wait_recv()
+    target = [jnp.sum(first[pl.ds(8 * l, 8)].astype(jnp.float32), axis=0) for l in range(2)]
+    share(2, second, at["z"], jnp.concatenate(target, axis=0).astype(second.dtype), along_z)
+    forward(2)
+    all_of(1, blocks.at[pl.ds(0, 6)]).wait_recv()
+    lay_out(0)
+    all_of(13, blocks.at[pl.ds(0, 6)]).wait_recv()
+    lay_out(1)
     left = [wide[l, :32] for l in range(2)]
     right = [wide[l, 32:] for l in range(2)]
     all_of(2, second.at[pl.ds(0, 7)]).wait_recv()
@@ -293,7 +298,8 @@
     out_ref[1:2] = residual - alpha * image
 
     all_of(0, first.at[pl.ds(0, 15)]).wait_send()
-    all_of(1, blocks.at[pl.ds(0, 12)]).wait_send()
+    all_of(1, blocks.at[pl.ds(0, 6)]).wait_send()
+    all_of(13, blocks.at[pl.ds(0, 6)]).wait_send()
     for d in (1, 2, 3):
         all_of(9 + d, blocks.at[0]).wait_send()
     all_of(2, second.at[pl.ds(0, 7)]).wait_send()
@@ -335,8 +341,8 @@
             pltpu.VMEM((2, 1, 3 * LANES), jnp.float32),
             pltpu.SemaphoreType.DMA((CHUNKS, 4)),
             pltpu.SemaphoreType.DMA,
-            pltpu.SemaphoreType.DMA((13,)),
-            pltpu.SemaphoreType.DMA((13,)),
+            pltpu.SemaphoreType.DMA((14,)),
+            pltpu.SemaphoreType.DMA((14,)),
         ],
         compiler_params=pltpu.CompilerParams(
             collective_id=0, has_side_effects=True, vmem_limit_bytes=32 * 2**20

time: 33.6 us -> 33.2 us (0.988)
    pallas_call x1, Pallas kernels: 32.3 us -> 32 us  [per_device(): pl.pallas_call(functools.partial(kernel, rows, rank, total_features, val_...]
where the time goes in v6:
time: 33.2 us; the launch traced here: 33.1 us
  Pallas kernels  32 us (96%)
  between operations  0.64 us (2%)
  local copies, waits for them, and re-layouts  0.52 us (2%)
    pallas_call x1, Pallas kernels, per_device(): pl.pallas_call(functools.partial(kernel, rows, rank, total_features, val_...  32 us

profile of v6, /device:TPU:1, one launch (start us, length us, event | category | flops | bytes accessed | tf_op | source)
XLA Modules:
  0.0 33.1 jit_solution(7688879841452086396)
XLA Ops:
  0.6 32.0 %reweight.1 = f32[2,128]{1,0:T(2,128)S(1)} custom-call(bf16[1,26,4,5120]{3,2,1,0:T(4,128)(2,1)} %lf_hbm.1, bf16[1,26,4,5120]{3,2,1,0:T(4,128)(2,1)} %rf_hbm.1, bf16[1,32,5120]{2,1,0:T(8,128)(2,1)} %bitcast.7, bf16[1,64,5120]{2,1,0:T(8,128)(2,1)} %bitcast.6, s32[256]{0:T(256)} %ids_hbm.1), custom_call_target="tpu_custom_call" | custom-call | tf_op jit(solution)/shard_map/reweight/pallas_call | solution.py:322
  32.6 0.5 %slice_bitcast_fusion = (f32[26]{0:T(128)}, f32[26]{0:T(128)}) fusion(f32[2,128]{1,0:T(2,128)S(1)} %reweight.1), kind=kLoop, calls=%fused_computation | loop fusion | bytes 416 | tf_op jit(solution)/shard_map/squeeze | solution.py:352

commit v7 on v6

--- a/solution.py
+++ b/solution.py
@@ -51,8 +51,15 @@
     return jnp.concatenate([value[:16], value[16:]], axis=1)
 
 
-def unpack(value):
-    return jnp.concatenate([value[:, :64], value[:, 64:]], axis=0)
+def low_lanes(rows):
+    return lax.broadcasted_iota(jnp.int32, (rows, LANES), 1) < LANES // 2
+
+
+def side_by_side(first, second):
+    low = low_lanes(16)
+    top = jnp.where(low, first, pltpu.roll(second, LANES // 2, 1))
+    bottom = jnp.where(low, pltpu.roll(first, LANES // 2, 1), second)
+    return jnp.concatenate([top, bottom], axis=0)
 
 
 def dot(a, b, dims):
@@ -65,11 +72,11 @@
 
 
 def to_lanes(left, right, values, ranks=lambda term: term):
-    total = None
-    for l in range(2):
-        mixed = dot(split(unpack(values[l])), right[l], NN)
-        term = ranks((mixed[:32] + mixed[32:]) * left[l].astype(jnp.float32))
-        total = term if total is None else total + term
+    low = low_lanes(32)
+    both = jnp.concatenate([split(jnp.where(low, values, 0.0)), split(jnp.where(low, 0.0, values))], axis=0)
+    mixed = dot(both, right, NN)
+    total = ranks((mixed[:32] + mixed[32:64]) * left[0].astype(jnp.float32))
+    total += ranks((mixed[64:96] + mixed[96:]) * left[1].astype(jnp.float32))
     return jnp.sum(total, axis=0, keepdims=True)
 
 
@@ -83,7 +90,7 @@
 
 
 def products(a, b):
-    return jnp.sum(a[0] * b[0] + a[1] * b[1], axis=0, keepdims=True)
+    return jnp.sum(a * b, axis=0, keepdims=True)
 
 
 def halves(line):
@@ -98,7 +105,7 @@
 def kernel(
     rows, rank, total_features, val_count,
     lf_hbm, rf_hbm, lp_hbm, rp_hbm, ids_hbm, out_ref,
-    lf, rf, lp, rp, ids, blocks, wide, first, second, sums, norms, pair_0, pair_1, pair_2,
+    lf, rf, lp, rp, ids, blocks, wide_left, wide_right, first, second, sums, norms, pair_0, pair_1, pair_2,
     load_sem, ids_sem, send_sem, recv_sem,
 ):
     at = coordinates()
@@ -213,37 +220,38 @@
                     jnp.where(segment == 2, moves[2], moves[3]),
                 )
                 lanes = slice(256 * r + LANES * h, 256 * r + LANES * h + LANES)
-                wide[l, :, lanes] = value.astype(jnp.bfloat16)
+                wide_left[pl.ds(32 * l, 32), lanes] = value[:32].astype(jnp.bfloat16)
+                wide_right[pl.ds(64 * l, 64), lanes] = value[32:].astype(jnp.bfloat16)
 
     segment = lax.broadcasted_iota(jnp.int32, (96, LANES), 1) // GROUP
     forward(1)
     forward(3)
     all_of(0, first.at[pl.ds(0, 15)]).wait_recv()
     target = [jnp.sum(first[pl.ds(8 * l, 8)].astype(jnp.float32), axis=0) for l in range(2)]
-    share(2, second, at["z"], jnp.concatenate(target, axis=0).astype(second.dtype), along_z)
+    share(2, second, at["z"], side_by_side(*target).astype(second.dtype), along_z)
     forward(2)
     all_of(1, blocks.at[pl.ds(0, 6)]).wait_recv()
     lay_out(0)
     all_of(13, blocks.at[pl.ds(0, 6)]).wait_recv()
     lay_out(1)
-    left = [wide[l, :32] for l in range(2)]
-    right = [wide[l, 32:] for l in range(2)]
+    left = [wide_left[:32], wide_left[32:]]
+    right = wide_right[...]
     all_of(2, second.at[pl.ds(0, 7)]).wait_recv()
     target = jnp.sum(second[...].astype(jnp.float32), axis=0)
-    target = [target[:16], target[16:]]
 
     def all_ranks(line):
         line = jnp.concatenate([line] * 4, axis=1)
-        return [to_features(left[l], right[l], line) for l in range(2)]
+        both = jnp.concatenate([split(left[l].astype(jnp.float32) * line) for l in range(2)], axis=0)
+        parts = dot(both, right, NT)
+        return jnp.where(low_lanes(32), parts[:32] + parts[32:64], parts[64:96] + parts[96:])
 
     def send_features(index, values, scalars):
-        share(6 + index, sums.at[index], group_slot, jnp.concatenate(values, axis=0).astype(jnp.bfloat16), sharers)
+        share(6 + index, sums.at[index], group_slot, values.astype(jnp.bfloat16), sharers)
         share(8 + index, norms.at[index], group_slot, jnp.concatenate([halves(s) for s in scalars], axis=1), sharers)
 
     def take_features(index):
         all_of(6 + index, sums.at[index, pl.ds(0, 7)]).wait_recv()
-        whole = jnp.sum(sums[index].astype(jnp.float32), axis=0)
-        return [whole[:16], whole[16:]]
+        return jnp.sum(sums[index].astype(jnp.float32), axis=0)
 
     def take_norms(index):
         all_of(8 + index, norms.at[index, pl.ds(0, 7)]).wait_recv()
@@ -280,7 +288,7 @@
     start, residual, product = own_row(start), own_row(residual), own_row(product)
     weights = alpha * start
     left = [blocks[8 * l + own_slot, :32] for l in range(2)]
-    right = [blocks[8 * l + own_slot, 32:] for l in range(2)]
+    right = jnp.concatenate([blocks[8 * l + own_slot, 32:] for l in range(2)], axis=0)
 
     again = take_features(1)
     value = [to_lanes(left, right, again), products(again, again), products(again, mixed)]
@@ -331,7 +339,8 @@
             pltpu.VMEM((kb, width), jnp.bfloat16),
             pltpu.SMEM((val_count,), jnp.int32),
             pltpu.VMEM((16, ka + kb, LANES), jnp.bfloat16),
-            pltpu.VMEM((2, ka + kb, 8 * LANES), jnp.bfloat16),
+            pltpu.VMEM((2 * ka, 8 * LANES), jnp.bfloat16),
+            pltpu.VMEM((2 * kb, 8 * LANES), jnp.bfloat16),
             pltpu.VMEM((16, 16, LANES), jnp.bfloat16),
             pltpu.VMEM((8, 32, LANES), jnp.bfloat16),
             pltpu.VMEM((2, 8, 32, LANES), jnp.bfloat16),

time: 33.2 us -> 33.1 us (level)
  no operation moved by 1% of the time
where the time goes in v7:
time: 33.1 us; the launch traced here: 33 us
  Pallas kernels  31.9 us (96%)
  between operations  0.64 us (2%)
  local copies, waits for them, and re-layouts  0.52 us (2%)
    pallas_call x1, Pallas kernels, per_device(): pl.pallas_call(functools.partial(kernel, rows, rank, total_features, val_...  31.9 us

profile of v7, /device:TPU:1, one launch (start us, length us, event | category | flops | bytes accessed | tf_op | source)
XLA Modules:
  0.0 33.0 jit_solution(13956191678404576323)
XLA Ops:
  0.6 31.9 %reweight.1 = f32[2,128]{1,0:T(2,128)S(1)} custom-call(bf16[1,26,4,5120]{3,2,1,0:T(4,128)(2,1)} %lf_hbm.1, bf16[1,26,4,5120]{3,2,1,0:T(4,128)(2,1)} %rf_hbm.1, bf16[1,32,5120]{2,1,0:T(8,128)(2,1)} %bitcast.7, bf16[1,64,5120]{2,1,0:T(8,128)(2,1)} %bitcast.6, s32[256]{0:T(256)} %ids_hbm.1), custom_call_target="tpu_custom_call" | custom-call | tf_op jit(solution)/shard_map/reweight/pallas_call | solution.py:330
  32.5 0.5 %slice_bitcast_fusion = (f32[26]{0:T(128)}, f32[26]{0:T(128)}) fusion(f32[2,128]{1,0:T(2,128)S(1)} %reweight.1), kind=kLoop, calls=%fused_computation | loop fusion | bytes 416 | tf_op jit(solution)/shard_map/squeeze | solution.py:361

commit v8 on v7

--- a/solution.py
+++ b/solution.py
@@ -135,6 +135,8 @@
 
     greet(order)
 
+    load_ids = pltpu.make_async_copy(ids_hbm, ids, ids_sem)
+    load_ids.start()
     loads = []
     for i in range(CHUNKS):
         part = pl.ds(i * step, step)
@@ -147,8 +149,6 @@
         for copy in group:
             copy.start()
         loads.append(group)
-    load_ids = pltpu.make_async_copy(ids_hbm, ids, ids_sem)
-    load_ids.start()
     greet(rest)
 
     lane = lax.broadcasted_iota(jnp.int32, (8, LANES), 1) % GROUP
@@ -290,6 +290,17 @@
     left = [blocks[8 * l + own_slot, :32] for l in range(2)]
     right = jnp.concatenate([blocks[8 * l + own_slot, 32:] for l in range(2)], axis=0)
 
+    all_of(0, first.at[pl.ds(0, 15)]).wait_send()
+    all_of(1, blocks.at[pl.ds(0, 6)]).wait_send()
+    all_of(13, blocks.at[pl.ds(0, 6)]).wait_send()
+    for d in (1, 2, 3):
+        all_of(9 + d, blocks.at[0]).wait_send()
+    all_of(2, second.at[pl.ds(0, 7)]).wait_send()
+    all_of(3, pair_0.at[0]).wait_send()
+    all_of(4, pair_1.at[0]).wait_send()
+    all_of(6, sums.at[0, pl.ds(0, 7)]).wait_send()
+    all_of(8, norms.at[0, pl.ds(0, 7)]).wait_send()
+
     again = take_features(1)
     value = [to_lanes(left, right, again), products(again, again), products(again, mixed)]
     share(5, pair_2, at["c"], jnp.concatenate(value, axis=1), [other])
@@ -297,6 +308,8 @@
     beta = norm_next / norm
     direction = residual + beta * start
     length = norm_next + 2.0 * beta * cross + beta * beta * norm
+    all_of(7, sums.at[1, pl.ds(0, 7)]).wait_send()
+    all_of(9, norms.at[1, pl.ds(0, 7)]).wait_send()
     all_of(5, pair_2.at[0]).wait_recv()
     both = pair_2[0] + pair_2[1]
     square = total(both[:, LANES:2 * LANES]) + 2.0 * beta * total(both[:, 2 * LANES:]) + beta * beta * mixed_square
@@ -304,18 +317,7 @@
     image = (over_rank(both[:, :LANES]) + beta * product) * scale + RIDGE * direction
     out_ref[0:1] = weights + alpha * direction
     out_ref[1:2] = residual - alpha * image
-
-    all_of(0, first.at[pl.ds(0, 15)]).wait_send()
-    all_of(1, blocks.at[pl.ds(0, 6)]).wait_send()
-    all_of(13, blocks.at[pl.ds(0, 6)]).wait_send()
-    for d in (1, 2, 3):
-        all_of(9 + d, blocks.at[0]).wait_send()
-    all_of(2, second.at[pl.ds(0, 7)]).wait_send()
-    for i, pair in enumerate((pair_0, pair_1, pair_2)):
-        all_of(3 + i, pair.at[0]).wait_send()
-    for i in range(2):
-        all_of(6 + i, sums.at[i, pl.ds(0, 7)]).wait_send()
-        all_of(8 + i, norms.at[i, pl.ds(0, 7)]).wait_send()
+    all_of(5, pair_2.at[0]).wait_send()
 
 
 def per_device(left_factors, right_factors, left_proj, right_proj, val_ids):

time: 33.1 us -> 33.1 us (level)
  no operation moved by 1% of the time
where the time goes in v8:
time: 33.1 us; the launch traced here: 33 us
  Pallas kernels  31.8 us (96%)
  between operations  0.64 us (2%)
  local copies, waits for them, and re-layouts  0.52 us (2%)
    pallas_call x1, Pallas kernels, per_device(): pl.pallas_call(functools.partial(kernel, rows, rank, total_features, val_...  31.8 us

profile of v8, /device:TPU:1, one launch (start us, length us, event | category | flops | bytes accessed | tf_op | source)
XLA Modules:
  0.0 33.0 jit_solution(12057708405028480747)
XLA Ops:
  0.6 31.8 %reweight.1 = f32[2,128]{1,0:T(2,128)S(1)} custom-call(bf16[1,26,4,5120]{3,2,1,0:T(4,128)(2,1)} %lf_hbm.1, bf16[1,26,4,5120]{3,2,1,0:T(4,128)(2,1)} %rf_hbm.1, bf16[1,32,5120]{2,1,0:T(8,128)(2,1)} %bitcast.7, bf16[1,64,5120]{2,1,0:T(8,128)(2,1)} %bitcast.6, s32[256]{0:T(256)} %ids_hbm.1), custom_call_target="tpu_custom_call" | custom-call | tf_op jit(solution)/shard_map/reweight/pallas_call | solution.py:332
  32.5 0.5 %slice_bitcast_fusion = (f32[26]{0:T(128)}, f32[26]{0:T(128)}) fusion(f32[2,128]{1,0:T(2,128)S(1)} %reweight.1), kind=kLoop, calls=%fused_computation | loop fusion | bytes 416 | tf_op jit(solution)/shard_map/squeeze | solution.py:363
